TPU v7x, 32 devices: a whole 2x2x4 slice. The times are simulated.
32 devices in a mesh: perm: 2 (over y), subj: 8 (over z, core), vert: 2 (over x).
Axes of the slice: x: 2, y: 2, z: 4, core: 2. Of those that a mesh axis runs over, the one named last changes fastest.
Arguments:
- kinship: bfloat16 [2048, 2048], P('subj')
- phenotype: bfloat16 [2048, 2048], P('subj', 'vert')
- shuffle: int32 [4096], P(('perm', 'subj')), parts along dimension 0, may hold values from 0 to 2047, as said below
Outputs:
- statistic: float32 [4096], P(('perm', 'vert')), parts along dimension 0
There are 2 independent parts, one for each index of `perm`. A program takes and returns all parts, laid end to end along the dimension named above; an argument that names none is the same for every part. Nothing has to cross between parts.
Inputs may be any that keep to these rules, and one draw needn't show every extreme that they name: shuffle is a permutation of 0 to 2047 that maps every subject into its own exchangeability block.
All inputs are finite; a program needn't handle non-finite values.
Results may differ from a plain program's by a relative error of at most 0.0003.
Values may be sent and summed in bfloat16 or wider, within the bound.
No kernel may reach another device: no remote copies, remote signals or barrier semaphores. Data moves between devices by JAX's collectives and lax.ppermute only.
A program may use at most 128 MiB of HBM per device.

v0:
```python
import jax
import jax.numpy as jnp
from jax import lax
from jax.sharding import PartitionSpec as P


def per_device(kinship, phenotype, shuffle):
    row_count = phenotype.shape[0]
    subject_count = kinship.shape[1]
    row_offset = lax.axis_index("subj") * row_count
    shuffle_all = lax.all_gather(shuffle, "subj", axis=0, tiled=True)
    own_block = lax.dynamic_slice_in_dim(kinship, row_offset, row_count, 1)
    kin_diag = jnp.diagonal(own_block).astype(jnp.float32)
    inverse = (
        jnp.zeros((subject_count,), jnp.int32)
        .at[shuffle_all]
        .set(jnp.arange(subject_count, dtype=jnp.int32))
    )
    kin_moved = jnp.take(kinship, inverse, axis=1)
    piece = lax.all_gather(phenotype, "subj", axis=0, tiled=True)
    piece_rows = piece.shape[0]
    targets = jnp.arange(piece_rows, dtype=jnp.int32)
    picker = (shuffle[:, None] == targets[None, :]).astype(jnp.bfloat16)
    product = jnp.dot(kin_moved, piece, preferred_element_type=jnp.float32)
    picked = jnp.dot(picker, piece, preferred_element_type=jnp.float32)
    local_perm = picked.astype(jnp.bfloat16)
    moved = local_perm.astype(jnp.float32)
    cross_term = jnp.sum(moved * (product - kin_diag[:, None] * moved), axis=0)
    values = phenotype.astype(jnp.float32)
    squares = jnp.sum(values * values, axis=0)
    cross_all, squares_all = lax.psum((cross_term, squares), "subj")
    return cross_all / (
        jnp.sqrt(jnp.float32(subject_count)) * (squares_all / subject_count + 1e-05)
    )


def solution(mesh):
    in_specs = (P("subj", None), P("subj", "vert"), P(("perm", "subj")))
    out_specs = P(("perm", "vert"))
    return jax.shard_map(
        per_device, mesh=mesh, in_specs=in_specs, out_specs=out_specs, check_vma=False
    )
```

profile of v0, /device:TPU:0, one launch (start us, length us, event | category | flops | bytes accessed | tf_op | source)
XLA Modules:
  0.0 86.2 jit_solution(4435707539312031258)
XLA Ops:
  6.5 0.0 all-gather.3.cloned.1.call-start
  6.5 0.7 all-gather.3.cloned.1.call-update
  7.3 1.5 %copy.6 = bf16[256,2048]{0,1:T(8,128)(2,1)S(1)} copy(bf16[256,2048]{1,0:T(8,128)(2,1)} %param.3) | data formatting | bytes 2097152 | tf_op args[0]
  8.8 0.9 %constant_dynamic-slice_fusion = bf16[256,256]{1,0:T(8,128)(2,1)S(1)} fusion(bf16[256,2048]{1,0:T(8,128)(2,1)} %param.3, s32[]{:T(128)S(6)} %select_n.22), kind=kLoop, calls=%fused_computation.23 | loop fusion | bytes 262148 | tf_op jit(solution)/shard_map/dynamic_slice | solution.py:12
  9.7 2.5 %gather_fusion.1 = bf16[256]{0:T(256)(128)(2,1)S(1)} fusion(bf16[256,256]{1,0:T(8,128)(2,1)S(1)} %constant_dynamic-slice_fusion, s32[256]{0:T(256)S(1)} %bitcast.5), kind=kCustom, calls=%fused_computation.1 | custom fusion | bytes 3072 | tf_op jit(solution)/shard_map/jit(diagonal)/cond/branch_0_fun/gather | solution.py:13
  12.2 13.7 %all-gather = s32[8,1,256]{2,1,0:T(1,128)S(1)} all-gather(s32[1,1,256]{2,1,0:T(1,128)} %bitcast.7), channel_id=1, replica_groups=mesh['perm'=2,'subj'=8,'vert'=2] {'subj'}, dimensions={0}, use_global_device_ids=true | all-gather | bytes 9216 | tf_op jit(solution)/shard_map/all_gather | solution.py:11
  25.9 8.0 %scatter_custom_fusion = s32[2048]{0:T(1024)S(1)} fusion(s32[2048]{0:T(1024)S(1)} %compare_select_fusion.1, s32[2048]{0:T(1024)S(1)} %iota.16, s32[]{:T(128)} %constant.12.clone.1), kind=kCustom, calls=%fused_computation.20 | custom fusion | bytes 8196 | tf_op jit(solution)/shard_map/scatter | solution.py:17
  34.0 0.0 copy-start
  34.0 0.0 copy-start.1
  34.0 7.5 %gather_fusion = bf16[2048,256]{1,0:T(8,128)(2,1)S(1)} fusion(bf16[256,2048]{0,1:T(8,128)(2,1)S(1)} %copy.6, s32[2048]{0:T(1024)S(1)} %fusion.7), kind=kCustom, calls=%fused_computation | custom fusion | bytes 2105344 | tf_op jit(solution)/shard_map/jit(_take)/gather | solution.py:19
  41.5 0.0 copy-done
  41.6 0.1 multiply_reduce_fusion
  41.7 17.1 %all-gather.3.cloned.1.call-done = bf16[2048,1024]{1,0:T(8,128)(2,1)} async-done(((bf16[256,1024]{1,0:T(8,128)(2,1)}), bf16[2048,1024]{1,0:T(8,128)(2,1)}) %all-gather.3.cloned.1.call-update) | async-done | bytes 4194320 | tf_op jit(solution)/shard_map/all_gather | solution.py:20
  58.8 0.0 copy-done.1
  58.8 0.0 copy-start.2
  58.8 3.6 %fusion.1 = bf16[256,1024]{1,0:T(8,128)(2,1)S(1)} fusion(bf16[2048,1024]{1,0:T(8,128)(2,1)} %all-gather.3.cloned.1.call-done, s32[256]{0:T(256)S(1)} %copy-done.1), kind=kOutput, calls=%fused_computation.8 | convolution fusion | flops 1074528256 | bytes 4719616 | tf_op jit(solution)/shard_map/dot_general | solution.py:25
  62.5 0.0 copy-done.2
  62.5 1.5 %fusion.2 = f32[1024]{0:T(1024)S(1)} fusion(bf16[2048,1024]{1,0:T(8,128)(2,1)S(1)} %copy-done.2, bf16[256,1024]{1,0:T(8,128)(2,1)S(1)} %fusion.1, bf16[2048,256]{1,0:T(8,128)(2,1)S(1)} %gather_fusion, pred[2048]{0:T(1024)(128)(4,1)S(1)} %compare_and_fusion, f32[256]{0:T(256)S(1)} %convert_element_type.19), kind=kOutput, calls=%fused_computation.9 | convolution fusion | flops 1075575808 | bytes 5774336 | tf_op jit(solution)/shard_map/dot_general | solution.py:24
  63.9 14.9 %all-reduce = (f32[1024]{0:T(1024)S(1)}, f32[1024]{0:T(1024)S(1)}) all-reduce(f32[1024]{0:T(1024)S(1)} %fusion.2, f32[1024]{0:T(1024)S(1)} %multiply_reduce_fusion), channel_id=1, replica_groups=mesh['perm'=2,'subj'=8,'vert'=2] {'subj'}, use_global_device_ids=true, to_apply=%region_2.3 | all-reduce | flops 2048 | bytes 16384 | tf_op jit(solution)/shard_map/psum | solution.py:31
  78.8 0.6 multiply_divide_fusion
  (6 shorter events, 0.0 us)
Async XLA Ops:
  6.5 52.3 %all-gather.3.cloned.1.call-start = ((), (), s32[]{:S(2)}) async-start(), calls=%async_computation | async-start | bytes 4718592 | tf_op jit(solution)/shard_map/all_gather | solution.py:20
  34.0 7.5 %copy-start = (bf16[256,1024]{1,0:T(8,128)(2,1)S(1)}, bf16[256,1024]{1,0:T(8,128)(2,1)}, u32[]{:S(2)}) copy-start(bf16[256,1024]{1,0:T(8,128)(2,1)} %param.4) | copy-start | bytes 1572868
  34.0 24.8 %copy-start.1 = (s32[256]{0:T(256)S(1)}, s32[256]{0:T(256)}, u32[]{:S(2)}) copy-start(s32[256]{0:T(256)} %param.5) | copy-start | bytes 3076
  58.8 3.6 %copy-start.2 = (bf16[2048,1024]{1,0:T(8,128)(2,1)S(1)}, bf16[2048,1024]{1,0:T(8,128)(2,1)}, u32[]{:S(2)}) copy-start(bf16[2048,1024]{1,0:T(8,128)(2,1)} %all-gather.3.cloned.1.call-done) | copy-start | bytes 12582916
Sparse Core Ops, SparseCore 0:
  9.0 49.8 all-gather.2
where the time goes:
time: 86.4 us; the launch traced here: 86.2 us
  blocking collectives  28.6 us (33%)
  local copies, waits for them, and re-layouts  20.5 us (24%)
  waiting for transfers between devices  17.8 us (21%)
  between operations  13.5 us (16%)
  matrix products  5.08 us (6%)
    all_gather x1, waiting for transfers between devices, per_device(): piece = lax.all_gather(phenotype, 'subj', axis=0, tiled=True)  17.1 us
    psum x1, blocking collectives, per_device(): cross_all, squares_all = lax.psum((cross_term, squares), 'subj')  14.9 us
    all_gather x1, blocking collectives, per_device(): shuffle_all = lax.all_gather(shuffle, 'subj', axis=0, tiled=True)  13.7 us
    scatter x1, local copies, waits for them, and re-layouts, per_device(): inverse = jnp.zeros((subject_count,), jnp.int32).at[shuffle_all].set(jnp....  8.05 us
    gather x1, local copies, waits for them, and re-layouts, per_device(): kin_moved = jnp.take(kinship, inverse, axis=1)  7.5 us
    dot_general x1, matrix products, per_device(): picked = jnp.dot(picker, piece, preferred_element_type=jnp.float32)  3.63 us
    gather x1, local copies, waits for them, and re-layouts, per_device(): kin_diag = jnp.diagonal(own_block).astype(jnp.float32)  2.49 us
  transfers between devices with their start and end apart: 1, of which 1 were waited for; matrix products, arithmetic and copies ran while one was open for 24% of the time, Pallas kernels for 0%

commit v1 on v0

v1 whole, which is shorter than its diff:
```python
import functools

import jax
import jax.numpy as jnp
from jax import lax
from jax.experimental import pallas as pl
from jax.experimental.pallas import tpu as pltpu
from jax.sharding import PartitionSpec as P

BF16, F32, I32 = jnp.bfloat16, jnp.float32, jnp.int32
LANES = 128


def in_vmem(x):
    return pltpu.with_memory_space_constraint(x, pltpu.VMEM)


def call(body, out, *args, flops=0):
    whole = pl.BlockSpec(memory_space=pltpu.VMEM)
    outs = [pltpu.VMEM(shape, dtype) for shape, dtype in out]
    size = sum(a.size * a.dtype.itemsize for a in args)
    return pl.pallas_call(
        body,
        out_shape=outs,
        in_specs=[whole] * len(args),
        out_specs=[whole] * len(outs),
        compiler_params=pltpu.CompilerParams(vmem_limit_bytes=16 << 20),
        cost_estimate=pl.CostEstimate(
            flops=flops, bytes_accessed=size, transcendentals=0
        ),
    )(*[in_vmem(a) for a in args])


def column_of(row):
    return jnp.transpose(jnp.broadcast_to(row, (LANES, row.shape[1])))


def picker(high, low, block, rows):
    shape = high.shape
    lane = lax.broadcasted_iota(I32, shape, 1)
    one, zero = jnp.ones(shape, BF16), jnp.zeros(shape, BF16)
    number = jnp.full(shape, block, F32).astype(BF16)
    inside = jnp.where(high == number, low, jnp.full(shape, -1, BF16))
    tiles = [
        jnp.where(inside == (lane + t).astype(F32).astype(BF16), one, zero)
        for t in range(0, rows, LANES)
    ]
    return jnp.concatenate(tiles, axis=1)


def split(column, rows):
    high = lax.div(column, rows)
    low = column - high * rows
    return high.astype(F32).astype(BF16), low.astype(F32).astype(BF16)


def square_rows(ref):
    v = ref[...].astype(F32)
    return jnp.sum(v * v, axis=0, keepdims=True)


def clear_diagonal(kin_ref, out_ref):
    rows = kin_ref.shape[0]
    first = pl.multiple_of(lax.axis_index("subj") * rows, LANES)
    out_ref[...] = kin_ref[...]
    r = lax.broadcasted_iota(I32, (rows, rows), 0)
    c = lax.broadcasted_iota(I32, (rows, rows), 1)
    own = kin_ref[:, pl.ds(first, rows)].astype(F32)
    out_ref[:, pl.ds(first, rows)] = jnp.where(r == c, 0.0, own).astype(BF16)


def move_rows(sources, shuffle_ref, *refs):
    n = len(sources)
    chunks, moved_ref, squares_ref = refs[:n], refs[n], refs[n + 1]
    rows, me = chunks[0].shape[0], lax.axis_index("subj")
    blocks = [me ^ s for s in sources]

    def tile(t, carry):
        high, low = split(column_of(shuffle_ref[pl.ds(t, 1), :]), rows)
        total = jnp.zeros((rows, chunks[0].shape[1]), F32)
        for block, chunk in zip(blocks, chunks):
            total += jnp.dot(
                picker(high, low, block, rows), chunk[...], preferred_element_type=F32
            )
        moved_ref[pl.ds(pl.multiple_of(t * rows, LANES), rows), :] = total.astype(BF16)
        return carry

    lax.fori_loop(0, shuffle_ref.shape[0], tile, 0, unroll=4)
    squares_ref[...] = sum(square_rows(c) for c in chunks)


def finish(sources, perms, shuffle_ref, moved_ref, squares_ref, own_ref, sib_ref, *refs):
    n = len(sources)
    chunks, out_ref, full_ref = refs[:n], refs[n], refs[n + 1]
    rows, me = chunks[0].shape[0], lax.axis_index("subj")
    blocks = [me ^ s for s in sources]
    tiles = shuffle_ref.shape[0]

    def tile(t, carry):
        high, low = split(column_of(shuffle_ref[pl.ds(t, 1), :]), rows)
        here = pl.ds(pl.multiple_of(t * rows, LANES), rows)
        total = moved_ref[here, :].astype(F32)
        for block, chunk in zip(blocks, chunks):
            total += jnp.dot(
                picker(high, low, block, rows), chunk[...], preferred_element_type=F32
            )
        full_ref[here, :] = total.astype(BF16)
        return carry

    lax.fori_loop(0, tiles, tile, 0, unroll=4)
    squares = squares_ref[...] + sum(square_rows(c) for c in chunks)
    subjects = tiles // perms * rows
    halves = squares.shape[1] // LANES
    dests = out_ref.shape[0] // perms
    for p in range(perms):
        x = full_ref[p * subjects : (p + 1) * subjects, :]
        cross = jnp.zeros_like(squares)
        for kin, block in ((own_ref, me), (sib_ref, me ^ 1)):
            product = jnp.dot(kin[...], x, preferred_element_type=F32)
            first = pl.multiple_of(p * subjects + block * rows, LANES)
            mine = full_ref[pl.ds(first, rows), :].astype(F32)
            cross += jnp.sum(mine * product, axis=0, keepdims=True)
        lines = [cross[:, h * LANES : (h + 1) * LANES] for h in range(halves)]
        lines += [squares[:, h * LANES : (h + 1) * LANES] for h in range(halves)]
        lines += [jnp.zeros((8 - 2 * halves, LANES), F32)]
        block = jnp.concatenate(lines, axis=0)
        for d in range(dests):
            out_ref[p * dests + d] = block


def per_device(n_perm, n_subj, kinship, phenotype, shuffle):
    rows, subjects = kinship.shape
    width = phenotype.shape[1] // (2 * n_perm)
    me = lax.axis_index("subj")
    core = lax.rem(me, 2)
    first = lax.axis_index("perm") * 2

    def exchange(x, mask):
        return lax.ppermute(x, "subj", [(i, i ^ mask) for i in range(n_subj)])

    mine = lax.dynamic_slice_in_dim(phenotype, (first + core) * width, width, 1)
    others = lax.dynamic_slice_in_dim(phenotype, (first + 1 - core) * width, width, 1)
    received = exchange(others, 1)
    own_kin = call(clear_diagonal, [((rows, subjects), BF16)], kinship)[0]
    sib_kin = exchange(own_kin, 1)

    everyone = jnp.broadcast_to(shuffle[None], (n_perm * n_subj, rows))
    shuffles = lax.all_to_all(everyone, ("perm", "subj"), 0, 0, tiled=True)

    chunks = [(0, mine), (1, received)]
    step = n_subj // 2
    while step > 1:
        chunks += [(s ^ step, exchange(x, step)) for s, x in chunks]
        step //= 2

    early, late = chunks[:-2], chunks[-2:]
    macs = shuffles.size * rows * width
    moved, squares = call(
        functools.partial(move_rows, [s for s, _ in early]),
        [((n_perm * subjects, width), BF16), ((1, width), F32)],
        shuffles,
        *[x for _, x in early],
        flops=2 * macs * len(early),
    )
    dests = n_perm * n_subj
    sums, _ = call(
        functools.partial(finish, [s for s, _ in late], n_perm),
        [((dests, 8, LANES), F32), ((n_perm * subjects, width), BF16)],
        shuffles,
        moved,
        squares,
        own_kin,
        sib_kin,
        *[x for _, x in late],
        flops=2 * macs * len(late) + 4 * n_perm * rows * subjects * width,
    )
    sums = lax.all_to_all(sums, ("perm", "subj"), 0, 0, tiled=True)
    sums = sums.reshape(n_perm, n_subj // 2, 2, 8, LANES)
    lines = width // LANES
    cross = jnp.sum(sums[:, :, :, :lines], axis=1)
    squares = sums[:, 0, :, lines : 2 * lines]
    count = jnp.float32(subjects)
    result = cross / (jnp.sqrt(count) * (squares / subjects + 1e-05))
    return result.reshape(-1)


def solution(mesh):
    in_specs = (P("subj", None), P("subj", "vert"), P(("perm", "subj")))
    out_specs = P(("perm", "vert"))
    body = functools.partial(per_device, mesh.shape["perm"], mesh.shape["subj"])
    return jax.shard_map(
        body, mesh=mesh, in_specs=in_specs, out_specs=out_specs, check_vma=False
    )
```

time: 86.4 us -> 47.2 us (0.55)
  local copies, waits for them, and re-layouts: 20.5 us -> 1.7 us
  waiting for transfers between devices: 17.8 us -> 1.92 us
  between operations: 13.5 us -> 0.06 us
  starting transfers between devices: 0.01 us -> 10.5 us
  Pallas kernels: 0 us -> 9.17 us
  blocking collectives: 28.6 us -> 23 us
  matrix products: 5.08 us -> 0 us
    all_to_all x0 -> x2, blocking collectives: none -> 23 us  [the longest x1 11.7 us: per_device(): shuffles = lax.all_to_all(everyone, ('perm', 'subj'), 0, 0, tiled=True)]
    all_gather x1 -> x0, waiting for transfers between devices: 17.1 us -> none  [per_device(): piece = lax.all_gather(phenotype, 'subj', axis=0, tiled=True)]
    psum x1 -> x0, blocking collectives: 14.9 us -> none  [per_device(): cross_all, squares_all = lax.psum((cross_term, squares), 'subj')]
    all_gather x1 -> x0, blocking collectives: 13.7 us -> none  [per_device(): shuffle_all = lax.all_gather(shuffle, 'subj', axis=0, tiled=True)]
    ppermute x0 -> x8, starting transfers between devices: none -> 10.5 us  [exchange(): return lax.ppermute(x, 'subj', [(i, i ^ mask) for i in range(n_subj)])]
    gather x2 -> x0, local copies, waits for them, and re-layouts: 9.99 us -> none  [the longest x1 7.5 us: per_device(): kin_moved = jnp.take(kinship, inverse, axis=1)]
    pallas_call x0 -> x3, Pallas kernels: none -> 9.17 us  [call(): pl.pallas_call(body, out_shape=outs, in_specs=[whole] * len(args), out_sp...]
    scatter x1 -> x0, local copies, waits for them, and re-layouts: 8.05 us -> none  [per_device(): inverse = jnp.zeros((subject_count,), jnp.int32).at[shuffle_all].set(jnp....]
  transfers between devices with their start and end apart: 1 -> 8, of which waited for: 1 -> 1; matrix products, arithmetic and copies ran while one was open for 24% -> 0% of each run, Pallas kernels for 0% -> 9%
where the time goes in v1:
time: 47.2 us; the launch traced here: 47 us
  blocking collectives  23 us (49%)
  starting transfers between devices  10.5 us (22%)
  Pallas kernels  9.17 us (19%)
  waiting for transfers between devices  1.92 us (4%)
  local copies, waits for them, and re-layouts  1.7 us (4%)
  other arithmetic  0.62 us (1%)
    all_to_all x1, blocking collectives, per_device(): shuffles = lax.all_to_all(everyone, ('perm', 'subj'), 0, 0, tiled=True)  11.7 us
    all_to_all x1, blocking collectives, per_device(): sums = lax.all_to_all(sums, ('perm', 'subj'), 0, 0, tiled=True)  11.3 us
    ppermute x8, starting transfers between devices, exchange(): return lax.ppermute(x, 'subj', [(i, i ^ mask) for i in range(n_subj)])  10.5 us
    pallas_call x3, Pallas kernels, call(): pl.pallas_call(body, out_shape=outs, in_specs=[whole] * len(args), out_sp...  9.17 us
    ppermute x8, waiting for transfers between devices, exchange(): return lax.ppermute(x, 'subj', [(i, i ^ mask) for i in range(n_subj)])  1.92 us
    unnamed x7, local copies, waits for them, and re-layouts  1.66 us
  transfers between devices with their start and end apart: 8, of which 1 were waited for; matrix products, arithmetic and copies ran while one was open for 0% of the time, Pallas kernels for 9%

profile of v1, /device:TPU:0, one launch (start us, length us, event | category | flops | bytes accessed | tf_op | source)
XLA Modules:
  0.0 47.0 jit_solution(6815891655801435977)
XLA Ops:
  0.0 0.0 copy-start
  0.0 1.2 %copy-done = bf16[256,2048]{1,0:T(8,128)(2,1)S(1)} copy-done((bf16[256,2048]{1,0:T(8,128)(2,1)S(1)}, bf16[256,2048]{1,0:T(8,128)(2,1)}, u32[]{:S(2)}) %copy-start) | copy-done | bytes 1048600
  1.2 0.0 copy-start.1
  1.2 0.0 copy-start.2
  1.2 0.1 shard_map.38.own_ref
  1.3 0.5 %collective-permute-start.5 = (bf16[256,2048]{1,0:T(8,128)(2,1)S(1)}, bf16[256,2048]{1,0:T(8,128)(2,1)S(1)}, u32[]{:S(2)}, u32[]{:S(2)}) collective-permute-start(bf16[256,2048]{1,0:T(8,128)(2,1)S(1)} %shard_map.38.own_ref), channel_id=1, source_target_pairs={{0,2},{2,0},{4,6},{6,4},{8,10},{10,8},{12,14},{14,12},{1,3},{3,1},... | collective-permute-start | bytes 3145736 | tf_op jit(solution)/shard_map/ppermute | solution.py:139
  1.8 0.4 copy-done.1
  2.3 0.5 %collective-permute-start = (bf16[256,256]{1,0:T(8,128)(2,1)S(1)}, bf16[256,256]{1,0:T(8,128)(2,1)S(1)}, u32[]{:S(2)}, u32[]{:S(2)}) collective-permute-start(bf16[256,256]{1,0:T(8,128)(2,1)S(1)} %get-tuple-element.11), channel_id=1, source_target_pairs={{0,2},{2,0},{4,6},{6,4},{8,10},{10,8},{12,14},{14,12},{1,3},{3,1},... | collective-permute-start | bytes 393224 | tf_op jit(solution)/shard_map/ppermute | solution.py:139
  2.8 3.7 %collective-permute-start.1 = (bf16[256,256]{1,0:T(8,128)(2,1)S(1)}, bf16[256,256]{1,0:T(8,128)(2,1)S(1)}, u32[]{:S(2)}, u32[]{:S(2)}) collective-permute-start(bf16[256,256]{1,0:T(8,128)(2,1)S(1)} %get-tuple-element.12.refs_0_), channel_id=1, source_target_pairs={{0,8},{2,10},{4,12},{6,14},{8,0},{10,2},{12,4},{14,6},{1,9},{3,11}... | collective-permute-start | bytes 393224 | tf_op jit(solution)/shard_map/ppermute | solution.py:139
  6.5 0.0 collective-permute-done.refs_1_
  6.5 1.8 %collective-permute-start.2 = (bf16[256,256]{1,0:T(8,128)(2,1)S(1)}, bf16[256,256]{1,0:T(8,128)(2,1)S(1)}, u32[]{:S(2)}, u32[]{:S(2)}) collective-permute-start(bf16[256,256]{1,0:T(8,128)(2,1)S(1)} %collective-permute-done.refs_1_), channel_id=1, source_target_pairs={{0,8},{2,10},{4,12},{6,14},{8,0},{10,2},{12,4},{14,6},{1,9},{3,11}... | collective-permute-start | bytes 393224 | tf_op jit(solution)/shard_map/ppermute | solution.py:139
  8.3 1.6 %collective-permute-start.3 = (bf16[256,256]{1,0:T(8,128)(2,1)S(1)}, bf16[256,256]{1,0:T(8,128)(2,1)S(1)}, u32[]{:S(2)}, u32[]{:S(2)}) collective-permute-start(bf16[256,256]{1,0:T(8,128)(2,1)S(1)} %get-tuple-element.12.refs_0_), channel_id=1, source_target_pairs={{0,4},{2,6},{4,0},{6,2},{8,12},{10,14},{12,8},{14,10},{1,5},{3,7},... | collective-permute-start | bytes 393224 | tf_op jit(solution)/shard_map/ppermute | solution.py:139
  9.9 0.4 collective-permute-start.4
  10.3 0.0 copy-done.2
  10.3 11.7 %all_to_all.13 = s32[16,1,256]{2,1,0:T(1,128)S(1)} all-to-all(s32[16,1,256]{2,1,0:T(1,128)S(1)} %broadcast_in_dim.2), channel_id=1, replica_groups=mesh['perm'=2,'subj'=8,'vert'=2] {'perm','subj'}, dimensions={0} | all-to-all | bytes 32768 | tf_op jit(solution)/shard_map/all_to_all | solution.py:148
  22.0 0.0 collective-permute-done.1.refs_2_
  22.0 0.0 collective-permute-start.6
  22.0 0.0 collective-permute-done.2.refs_3_
  22.1 2.0 %collective-permute-start.7 = (bf16[256,256]{1,0:T(8,128)(2,1)S(1)}, bf16[256,256]{1,0:T(8,128)(2,1)S(1)}, u32[]{:S(2)}, u32[]{:S(2)}) collective-permute-start(bf16[256,256]{1,0:T(8,128)(2,1)S(1)} %collective-permute-done.2.refs_3_), channel_id=1, source_target_pairs={{0,4},{2,6},{4,0},{6,2},{8,12},{10,14},{12,8},{14,10},{1,5},{3,7},... | collective-permute-start | bytes 393224 | tf_op jit(solution)/shard_map/ppermute | solution.py:139
  24.1 0.0 collective-permute-done.3.refs_4_
  24.1 0.0 collective-permute-done.4.refs_5_
  24.1 4.4 %shard_map.37 = (bf16[4096,256]{1,0:T(8,128)(2,1)S(1)}, f32[1,256]{1,0:T(1,128)S(1)}) custom-call(s32[16,256]{1,0:T(8,128)S(1)} %bitcast.6, bf16[256,256]{1,0:T(8,128)(2,1)S(1)} %get-tuple-element.12.refs_0_, bf16[256,256]{1,0:T(8,128)(2,1)S(1)} %collective-permute-done.refs_1_, bf16[256,256]{1,0:T(8,128)(2,1)S(1)} %collective-permute-done.1.refs_2_, ...), custom_call_target="tpu_custom_call" | custom-call | flops 3221225472 | bytes 802816 | tf_op jit(solution)/shard_map/pallas_call | solution.py:22
  28.5 0.0 collective-permute-done.6.refs_0_
  28.5 1.9 %collective-permute-done.7.refs_1_ = bf16[256,256]{1,0:T(8,128)(2,1)S(1)} collective-permute-done((bf16[256,256]{1,0:T(8,128)(2,1)S(1)}, bf16[256,256]{1,0:T(8,128)(2,1)S(1)}, u32[]{:S(2)}, u32[]{:S(2)}) %collective-permute-start.7) | collective-permute-done | bytes 131104 | tf_op jit(solution)/shard_map/ppermute | solution.py:139
  30.4 0.0 collective-permute-done.5.sib_ref
  30.4 4.7 %shard_map.39 = (f32[16,8,128]{2,1,0:T(8,128)S(1)}, bf16[4096,256]{1,0:T(8,128)(2,1)}) custom-call(s32[16,256]{1,0:T(8,128)S(1)} %bitcast.7, bf16[4096,256]{1,0:T(8,128)(2,1)S(1)} %get-tuple-element.8.moved_ref, f32[1,256]{1,0:T(1,128)S(1)} %get-tuple-element.9.squares_ref, bf16[256,2048]{1,0:T(8,128)(2,1)S(1)} %shard_map.38.own_ref, ...), custom_call_target="tpu_custom_call" | custom-call | flops 2147483648 | bytes 4473856 | tf_op jit(solution)/shard_map/pallas_call | solution.py:22
  35.1 11.3 %all_to_all.14 = f32[16,8,128]{2,1,0:T(8,128)S(1)} all-to-all(f32[16,8,128]{2,1,0:T(8,128)S(1)} %get-tuple-element.10), channel_id=1, replica_groups=mesh['perm'=2,'subj'=8,'vert'=2] {'perm','subj'}, dimensions={0} | all-to-all | bytes 131072 | tf_op jit(solution)/shard_map/all_to_all | solution.py:177
  46.4 0.6 %div.12 = f32[1024]{0:T(1024)} divide(f32[1024]{0:T(1024)S(1)} %bitcast.10, f32[1024]{0:T(1024)S(1)} %bitcast.11) | non-fusion elementwise | flops 1024 | bytes 12288 | tf_op jit(solution)/shard_map/div | solution.py:183
  (5 shorter events, 0.1 us)
Async XLA Ops:
  0.0 1.2 %copy-start = (bf16[256,2048]{1,0:T(8,128)(2,1)S(1)}, bf16[256,2048]{1,0:T(8,128)(2,1)}, u32[]{:S(2)}) copy-start(bf16[256,2048]{1,0:T(8,128)(2,1)} %kin_ref.1) | copy-start | bytes 3145732
  1.2 1.0 %copy-start.1 = (bf16[256,1024]{1,0:T(8,128)(2,1)S(1)}, bf16[256,1024]{1,0:T(8,128)(2,1)}, u32[]{:S(2)}) copy-start(bf16[256,1024]{1,0:T(8,128)(2,1)} %param.4) | copy-start | bytes 1572868
  1.2 9.1 %copy-start.2 = (s32[256]{0:T(256)S(1)}, s32[256]{0:T(256)}, u32[]{:S(2)}) copy-start(s32[256]{0:T(256)} %param.5) | copy-start | bytes 3076
  1.3 29.0 %collective-permute-start.5 = (bf16[256,2048]{1,0:T(8,128)(2,1)S(1)}, bf16[256,2048]{1,0:T(8,128)(2,1)S(1)}, u32[]{:S(2)}, u32[]{:S(2)}) collective-permute-start(bf16[256,2048]{1,0:T(8,128)(2,1)S(1)} %shard_map.38.own_ref), channel_id=1, source_target_pairs={{0,2},{2,0},{4,6},{6,4},{8,10},{10,8},{12,14},{14,12},{1,3},{3,1},... | collective-permute-start | bytes 3145736 | tf_op jit(solution)/shard_map/ppermute | solution.py:139
  2.3 4.2 %collective-permute-start = (bf16[256,256]{1,0:T(8,128)(2,1)S(1)}, bf16[256,256]{1,0:T(8,128)(2,1)S(1)}, u32[]{:S(2)}, u32[]{:S(2)}) collective-permute-start(bf16[256,256]{1,0:T(8,128)(2,1)S(1)} %get-tuple-element.11), channel_id=1, source_target_pairs={{0,2},{2,0},{4,6},{6,4},{8,10},{10,8},{12,14},{14,12},{1,3},{3,1},... | collective-permute-start | bytes 393224 | tf_op jit(solution)/shard_map/ppermute | solution.py:139
  2.8 19.2 %collective-permute-start.1 = (bf16[256,256]{1,0:T(8,128)(2,1)S(1)}, bf16[256,256]{1,0:T(8,128)(2,1)S(1)}, u32[]{:S(2)}, u32[]{:S(2)}) collective-permute-start(bf16[256,256]{1,0:T(8,128)(2,1)S(1)} %get-tuple-element.12.refs_0_), channel_id=1, source_target_pairs={{0,8},{2,10},{4,12},{6,14},{8,0},{10,2},{12,4},{14,6},{1,9},{3,11}... | collective-permute-start | bytes 393224 | tf_op jit(solution)/shard_map/ppermute | solution.py:139
  6.5 15.6 %collective-permute-start.2 = (bf16[256,256]{1,0:T(8,128)(2,1)S(1)}, bf16[256,256]{1,0:T(8,128)(2,1)S(1)}, u32[]{:S(2)}, u32[]{:S(2)}) collective-permute-start(bf16[256,256]{1,0:T(8,128)(2,1)S(1)} %collective-permute-done.refs_1_), channel_id=1, source_target_pairs={{0,8},{2,10},{4,12},{6,14},{8,0},{10,2},{12,4},{14,6},{1,9},{3,11}... | collective-permute-start | bytes 393224 | tf_op jit(solution)/shard_map/ppermute | solution.py:139
  8.3 15.8 %collective-permute-start.3 = (bf16[256,256]{1,0:T(8,128)(2,1)S(1)}, bf16[256,256]{1,0:T(8,128)(2,1)S(1)}, u32[]{:S(2)}, u32[]{:S(2)}) collective-permute-start(bf16[256,256]{1,0:T(8,128)(2,1)S(1)} %get-tuple-element.12.refs_0_), channel_id=1, source_target_pairs={{0,4},{2,6},{4,0},{6,2},{8,12},{10,14},{12,8},{14,10},{1,5},{3,7},... | collective-permute-start | bytes 393224 | tf_op jit(solution)/shard_map/ppermute | solution.py:139
  9.9 14.2 %collective-permute-start.4 = (bf16[256,256]{1,0:T(8,128)(2,1)S(1)}, bf16[256,256]{1,0:T(8,128)(2,1)S(1)}, u32[]{:S(2)}, u32[]{:S(2)}) collective-permute-start(bf16[256,256]{1,0:T(8,128)(2,1)S(1)} %collective-permute-done.refs_1_), channel_id=1, source_target_pairs={{0,4},{2,6},{4,0},{6,2},{8,12},{10,14},{12,8},{14,10},{1,5},{3,7},... | collective-permute-start | bytes 393224 | tf_op jit(solution)/shard_map/ppermute | solution.py:139
  22.0 6.4 %collective-permute-start.6 = (bf16[256,256]{1,0:T(8,128)(2,1)S(1)}, bf16[256,256]{1,0:T(8,128)(2,1)S(1)}, u32[]{:S(2)}, u32[]{:S(2)}) collective-permute-start(bf16[256,256]{1,0:T(8,128)(2,1)S(1)} %collective-permute-done.1.refs_2_), channel_id=1, source_target_pairs={{0,4},{2,6},{4,0},{6,2},{8,12},{10,14},{12,8},{14,10},{1,5},{3,7},... | collective-permute-start | bytes 393224 | tf_op jit(solution)/shard_map/ppermute | solution.py:139
  22.1 8.3 %collective-permute-start.7 = (bf16[256,256]{1,0:T(8,128)(2,1)S(1)}, bf16[256,256]{1,0:T(8,128)(2,1)S(1)}, u32[]{:S(2)}, u32[]{:S(2)}) collective-permute-start(bf16[256,256]{1,0:T(8,128)(2,1)S(1)} %collective-permute-done.2.refs_3_), channel_id=1, source_target_pairs={{0,4},{2,6},{4,0},{6,2},{8,12},{10,14},{12,8},{14,10},{1,5},{3,7},... | collective-permute-start | bytes 393224 | tf_op jit(solution)/shard_map/ppermute | solution.py:139

commit v2 on v0

v2 whole, which is shorter than its diff:
```python
import functools

import jax
import jax.numpy as jnp
from jax import lax
from jax.experimental import pallas as pl
from jax.experimental.pallas import tpu as pltpu
from jax.sharding import PartitionSpec as P

BF16, F32, I32 = jnp.bfloat16, jnp.float32, jnp.int32
LANES = 128


def call(body, out, *args, flops=0, scratch=(), from_hbm=0):
    space = [pltpu.HBM if i < from_hbm else pltpu.VMEM for i in range(len(args))]
    outs = [pltpu.VMEM(shape, dtype) for shape, dtype in out]
    size = sum(a.size * a.dtype.itemsize for a in args)
    return pl.pallas_call(
        body,
        out_shape=outs,
        in_specs=[pl.BlockSpec(memory_space=s) for s in space],
        out_specs=[pl.BlockSpec(memory_space=pltpu.VMEM)] * len(outs),
        scratch_shapes=scratch,
        compiler_params=pltpu.CompilerParams(vmem_limit_bytes=24 << 20),
        cost_estimate=pl.CostEstimate(
            flops=flops, bytes_accessed=size, transcendentals=0
        ),
    )(*[pltpu.with_memory_space_constraint(a, s) for a, s in zip(args, space)])


def dot(a, b):
    return jnp.dot(a, b, preferred_element_type=F32)


def tile_of(index, rows):
    return pl.ds(pl.multiple_of(index * rows, LANES), rows)


def square_rows(ref):
    v = ref[...].astype(F32)
    return jnp.sum(v * v, axis=0, keepdims=True)


def cut(
    order, phen_ref, kin_ref, shuffle_ref, mine_ref, others_ref, own_ref, sib_ref,
    everyone_ref, all_ref, line_ref, sems,
):
    rows, width = mine_ref.shape
    me = lax.axis_index("subj")
    core, first = lax.rem(me, 2), lax.axis_index("perm") * 2
    copies = [
        pltpu.make_async_copy(
            phen_ref.at[:, tile_of(first + core, width)], mine_ref, sems.at[0]
        ),
        pltpu.make_async_copy(
            phen_ref.at[:, tile_of(first + 1 - core, width)], others_ref, sems.at[1]
        ),
        pltpu.make_async_copy(kin_ref, all_ref, sems.at[2]),
        pltpu.make_async_copy(shuffle_ref, line_ref, sems.at[3]),
    ]
    for copy in copies:
        copy.start()
    for copy in copies:
        copy.wait()
    everyone_ref[...] = jnp.broadcast_to(line_ref[...], everyone_ref.shape)
    r = lax.broadcasted_iota(I32, (rows, rows), 0)
    c = lax.broadcasted_iota(I32, (rows, rows), 1)
    for i, source in enumerate(order):
        block = all_ref[:, tile_of(me ^ source, rows)]
        if source == 0:
            block = jnp.where(r == c, 0.0, block.astype(F32)).astype(BF16)
        j = order.index(source ^ 1)
        own_ref[:, i * rows : (i + 1) * rows] = block
        sib_ref[:, j * rows : (j + 1) * rows] = block


def columns_of(shuffle_ref, row, rows):
    line = jnp.broadcast_to(shuffle_ref[row : row + 1, :], (LANES, rows))
    column = jnp.transpose(line)
    high = lax.div(column, rows)
    low = column - high * rows
    return high.astype(F32).astype(BF16), low.astype(F32).astype(BF16)


def picker(digits, block, rows):
    high, low = digits
    shape = high.shape
    lane = lax.broadcasted_iota(I32, shape, 1)
    one, zero = jnp.ones(shape, BF16), jnp.zeros(shape, BF16)
    number = jnp.full(shape, block, F32).astype(BF16)
    inside = jnp.where(high == number, low, jnp.full(shape, -1, BF16))
    tiles = [
        jnp.where(inside == (lane + t).astype(F32).astype(BF16), one, zero)
        for t in range(0, rows, LANES)
    ]
    return jnp.concatenate(tiles, axis=1)


def find(order, chunks, digits, rows):
    me = lax.axis_index("subj")
    parts = [dot(picker(digits, me ^ s, rows), c[...]) for s, c in zip(order, chunks)]
    return sum(parts).astype(BF16)


def line_of(ref, perm, subj, perms):
    return ref[pl.ds(perm * (ref.shape[0] // perms) + subj, 1), :]


def square(a_ref, b_ref, out_ref):
    out_ref[...] = square_rows(a_ref) + square_rows(b_ref)


def move(order, perms, shuffle_ref, some_ref, *refs):
    chunks, (moved_ref, squares_ref) = refs[:-2], refs[-2:]
    rows, me = chunks[0].shape[0], lax.axis_index("subj")
    n = len(order)
    for p in range(perms):
        for i in range(n):
            digits = columns_of(line_of(shuffle_ref, p, me ^ order[i], perms), 0, rows)
            at = (p * n + i) * rows
            moved_ref[at : at + rows, :] = find(order, chunks, digits, rows)
    squares_ref[...] = some_ref[...] + sum(square_rows(c) for c in chunks[2:])


def add_block(order, which, perms, shuffle_ref, moved_ref, squares_ref, chunk_ref, *refs):
    moved_out, squares_out = refs
    rows, me = chunk_ref.shape[0], lax.axis_index("subj")
    n = len(order)
    for p in range(perms):
        for i in range(n):
            digits = columns_of(line_of(shuffle_ref, p, me ^ order[i], perms), 0, rows)
            here = slice((p * n + i) * rows, (p * n + i + 1) * rows)
            found = find([order[which]], [chunk_ref], digits, rows)
            moved_out[here, :] = moved_ref[here, :] + found
    squares_out[...] = squares_ref[...] + square_rows(chunk_ref)


def finish(order, perms, shuffle_ref, moved_ref, squares_ref, own_ref, sib_ref, last_ref, *refs):
    out_ref, full_ref = refs
    rows, me = last_ref.shape[0], lax.axis_index("subj")
    n = len(order)
    squares = squares_ref[...] + square_rows(last_ref)
    halves = squares.shape[1] // LANES
    dests = out_ref.shape[0] // perms
    for p in range(perms):
        for i in range(n):
            digits = columns_of(line_of(shuffle_ref, p, me ^ order[i], perms), 0, rows)
            here = slice((p * n + i) * rows, (p * n + i + 1) * rows)
            found = find(order[-1:], [last_ref], digits, rows)
            full_ref[i * rows : (i + 1) * rows, :] = moved_ref[here, :] + found
        cross = jnp.zeros_like(squares)
        for g, kin in enumerate((own_ref, sib_ref)):
            product = dot(kin[...], full_ref[...])
            mine = full_ref[g * rows : (g + 1) * rows, :].astype(F32)
            cross += jnp.sum(mine * product, axis=0, keepdims=True)
        lines = [cross[:, h * LANES : (h + 1) * LANES] for h in range(halves)]
        lines += [squares[:, h * LANES : (h + 1) * LANES] for h in range(halves)]
        lines += [jnp.zeros((8 - 2 * halves, LANES), F32)]
        block = jnp.concatenate(lines, axis=0)
        for d in range(dests):
            out_ref[p * dests + d] = block


def per_device(n_perm, n_subj, kinship, phenotype, shuffle):
    rows, subjects = kinship.shape
    width = phenotype.shape[1] // (2 * n_perm)

    def exchange(x, mask):
        return lax.ppermute(x, "subj", [(i, i ^ mask) for i in range(n_subj)])

    order, step = [0, 1], n_subj // 2
    while step > 1:
        order = order + [s ^ step for s in order]
        step //= 2

    mine, others, own_kin, for_sib, everyone = call(
        functools.partial(cut, order),
        [((rows, width), BF16)] * 2
        + [((rows, subjects), BF16)] * 2
        + [((n_perm * n_subj, rows), I32)],
        phenotype,
        kinship,
        shuffle[None],
        from_hbm=3,
        scratch=[
            pltpu.VMEM((rows, subjects), BF16),
            pltpu.VMEM((1, rows), I32),
            pltpu.SemaphoreType.DMA((4,)),
        ],
    )
    received = exchange(others, 1)
    sib_kin = exchange(for_sib, 1)
    shuffles = lax.all_to_all(everyone, ("perm", "subj"), 0, 0, tiled=True)

    chunks, step = [mine, received], n_subj // 2
    while step > 1:
        chunks = chunks + [exchange(x, step) for x in chunks]
        step //= 2

    table = [((n_perm * subjects, width), BF16), ((1, width), F32)]
    unit = 2 * rows * rows * width
    tiles = n_perm * n_subj
    squares = call(square, [((1, width), F32)], mine, received)[0]
    moved, squares = call(
        functools.partial(move, order, n_perm),
        table,
        shuffles,
        squares,
        *chunks[:-2],
        flops=unit * tiles * (n_subj - 2),
    )
    moved, squares = call(
        functools.partial(add_block, order, -2, n_perm),
        table,
        shuffles,
        moved,
        squares,
        chunks[-2],
        flops=unit * tiles,
    )
    sums = call(
        functools.partial(finish, order, n_perm),
        [((tiles, 8, LANES), F32)],
        shuffles,
        moved,
        squares,
        own_kin,
        sib_kin,
        chunks[-1],
        flops=unit * tiles * 3,
        scratch=[pltpu.VMEM((subjects, width), BF16)],
    )[0]
    sums = lax.all_to_all(sums, ("perm", "subj"), 0, 0, tiled=True)
    sums = sums.reshape(n_perm, n_subj // 2, 2, 8, LANES)
    lines = width // LANES
    cross = jnp.sum(sums[:, :, :, :lines], axis=1)
    squares = sums[:, 0, :, lines : 2 * lines]
    count = jnp.float32(subjects)
    result = cross / (jnp.sqrt(count) * (squares / subjects + 1e-05))
    return result.reshape(-1)


def solution(mesh):
    in_specs = (P("subj", None), P("subj", "vert"), P(("perm", "subj")))
    out_specs = P(("perm", "vert"))
    body = functools.partial(per_device, mesh.shape["perm"], mesh.shape["subj"])
    return jax.shard_map(
        body, mesh=mesh, in_specs=in_specs, out_specs=out_specs, check_vma=False
    )
```

time: 86.4 us -> 44.4 us (0.51)
  local copies, waits for them, and re-layouts: 20.5 us -> 0.02 us
  waiting for transfers between devices: 17.8 us -> 1.42 us
  between operations: 13.5 us -> 0.07 us
  starting transfers between devices: 0.01 us -> 11 us
  Pallas kernels: 0 us -> 8.92 us
  blocking collectives: 28.6 us -> 22.1 us
  matrix products: 5.08 us -> 0 us
    all_to_all x0 -> x2, blocking collectives: none -> 22.1 us  [the longest x1 11.7 us: per_device(): shuffles = lax.all_to_all(everyone, ('perm', 'subj'), 0, 0, tiled=True)]
    all_gather x1 -> x0, waiting for transfers between devices: 17.1 us -> none  [per_device(): piece = lax.all_gather(phenotype, 'subj', axis=0, tiled=True)]
    psum x1 -> x0, blocking collectives: 14.9 us -> none  [per_device(): cross_all, squares_all = lax.psum((cross_term, squares), 'subj')]
    all_gather x1 -> x0, blocking collectives: 13.7 us -> none  [per_device(): shuffle_all = lax.all_gather(shuffle, 'subj', axis=0, tiled=True)]
    ppermute x0 -> x8, starting transfers between devices: none -> 11 us  [exchange(): return lax.ppermute(x, 'subj', [(i, i ^ mask) for i in range(n_subj)])]
    gather x2 -> x0, local copies, waits for them, and re-layouts: 9.99 us -> none  [the longest x1 7.5 us: per_device(): kin_moved = jnp.take(kinship, inverse, axis=1)]
    pallas_call x0 -> x5, Pallas kernels: none -> 8.92 us  [call(): pl.pallas_call(body, out_shape=outs, in_specs=[pl.BlockSpec(memory_space=...]
    scatter x1 -> x0, local copies, waits for them, and re-layouts: 8.05 us -> none  [per_device(): inverse = jnp.zeros((subject_count,), jnp.int32).at[shuffle_all].set(jnp....]
  transfers between devices with their start and end apart: 1 -> 8, of which waited for: 1 -> 2; matrix products, arithmetic and copies ran while one was open for 24% -> 0% of each run, Pallas kernels for 0% -> 11%
where the time goes in v2:
time: 44.4 us; the launch traced here: 44.2 us
  blocking collectives  22.1 us (50%)
  starting transfers between devices  11 us (25%)
  Pallas kernels  8.92 us (20%)
  waiting for transfers between devices  1.42 us (3%)
  other arithmetic  0.62 us (1%)
    all_to_all x1, blocking collectives, per_device(): shuffles = lax.all_to_all(everyone, ('perm', 'subj'), 0, 0, tiled=True)  11.7 us
    ppermute x8, starting transfers between devices, exchange(): return lax.ppermute(x, 'subj', [(i, i ^ mask) for i in range(n_subj)])  11 us
    all_to_all x1, blocking collectives, per_device(): sums = lax.all_to_all(sums, ('perm', 'subj'), 0, 0, tiled=True)  10.4 us
    pallas_call x5, Pallas kernels, call(): pl.pallas_call(body, out_shape=outs, in_specs=[pl.BlockSpec(memory_space=...  8.92 us
    ppermute x8, waiting for transfers between devices, exchange(): return lax.ppermute(x, 'subj', [(i, i ^ mask) for i in range(n_subj)])  1.42 us
  transfers between devices with their start and end apart: 8, of which 2 were waited for; matrix products, arithmetic and copies ran while one was open for 0% of the time, Pallas kernels for 11%

profile of v2, /device:TPU:0, one launch (start us, length us, event | category | flops | bytes accessed | tf_op | source)
XLA Modules:
  0.0 44.2 jit_solution(7009735708960962147)
XLA Ops:
  0.0 1.6 %shard_map.37 = (bf16[256,256]{1,0:T(8,128)(2,1)S(1)}, bf16[256,256]{1,0:T(8,128)(2,1)S(1)}, bf16[256,2048]{1,0:T(8,128)(2,1)S(1)}, bf16[256,2048]{1,0:T(8,128)(2,1)S(1)}, s32[16,256]{1,0:T(8,128)S(1)}) custom-call(bf16[256,1024]{1,0:T(8,128)(2,1)} %phen_ref.1, bf16[256,2048]{1,0:T(8,128)(2,1)} %kin_ref.1, s32[1,256]{1,0:T(1,128)} %bitcast.16), custom_call_target="tpu_custom_call" | custom-call | bytes 1573888 | tf_op jit(solution)/shard_map/pallas_call | solution.py:18
  1.6 0.5 %collective-permute-start.6 = (bf16[256,2048]{1,0:T(8,128)(2,1)S(1)}, bf16[256,2048]{1,0:T(8,128)(2,1)S(1)}, u32[]{:S(2)}, u32[]{:S(2)}) collective-permute-start(bf16[256,2048]{1,0:T(8,128)(2,1)S(1)} %get-tuple-element.22), channel_id=1, source_target_pairs={{0,2},{2,0},{4,6},{6,4},{8,10},{10,8},{12,14},{14,12},{1,3},{3,1},... | collective-permute-start | bytes 3145736 | tf_op jit(solution)/shard_map/ppermute | solution.py:169
  2.1 0.1 collective-permute-start
  2.2 4.0 %collective-permute-start.1 = (bf16[256,256]{1,0:T(8,128)(2,1)S(1)}, bf16[256,256]{1,0:T(8,128)(2,1)S(1)}, u32[]{:S(2)}, u32[]{:S(2)}) collective-permute-start(bf16[256,256]{1,0:T(8,128)(2,1)S(1)} %get-tuple-element.15.a_ref.refs_0_), channel_id=1, source_target_pairs={{0,8},{2,10},{4,12},{6,14},{8,0},{10,2},{12,4},{14,6},{1,9},{3,11}... | collective-permute-start | bytes 393224 | tf_op jit(solution)/shard_map/ppermute | solution.py:169
  6.2 0.0 collective-permute-done.b_ref.refs_1_
  6.2 2.3 %collective-permute-start.2 = (bf16[256,256]{1,0:T(8,128)(2,1)S(1)}, bf16[256,256]{1,0:T(8,128)(2,1)S(1)}, u32[]{:S(2)}, u32[]{:S(2)}) collective-permute-start(bf16[256,256]{1,0:T(8,128)(2,1)S(1)} %collective-permute-done.b_ref.refs_1_), channel_id=1, source_target_pairs={{0,8},{2,10},{4,12},{6,14},{8,0},{10,2},{12,4},{14,6},{1,9},{3,11}... | collective-permute-start | bytes 393224 | tf_op jit(solution)/shard_map/ppermute | solution.py:169
  8.5 1.6 %collective-permute-start.3 = (bf16[256,256]{1,0:T(8,128)(2,1)S(1)}, bf16[256,256]{1,0:T(8,128)(2,1)S(1)}, u32[]{:S(2)}, u32[]{:S(2)}) collective-permute-start(bf16[256,256]{1,0:T(8,128)(2,1)S(1)} %get-tuple-element.15.a_ref.refs_0_), channel_id=1, source_target_pairs={{0,4},{2,6},{4,0},{6,2},{8,12},{10,14},{12,8},{14,10},{1,5},{3,7},... | collective-permute-start | bytes 393224 | tf_op jit(solution)/shard_map/ppermute | solution.py:169
  10.1 0.4 %collective-permute-start.4 = (bf16[256,256]{1,0:T(8,128)(2,1)S(1)}, bf16[256,256]{1,0:T(8,128)(2,1)S(1)}, u32[]{:S(2)}, u32[]{:S(2)}) collective-permute-start(bf16[256,256]{1,0:T(8,128)(2,1)S(1)} %collective-permute-done.b_ref.refs_1_), channel_id=1, source_target_pairs={{0,4},{2,6},{4,0},{6,2},{8,12},{10,14},{12,8},{14,10},{1,5},{3,7},... | collective-permute-start | bytes 393224 | tf_op jit(solution)/shard_map/ppermute | solution.py:169
  10.6 11.7 %all_to_all.16 = s32[16,1,256]{2,1,0:T(1,128)S(1)} all-to-all(s32[16,1,256]{2,1,0:T(1,128)S(1)} %copy.4), channel_id=1, replica_groups=mesh['perm'=2,'subj'=8,'vert'=2] {'perm','subj'}, dimensions={0} | all-to-all | bytes 32768 | tf_op jit(solution)/shard_map/all_to_all | solution.py:193
  22.3 0.0 collective-permute-done.1.refs_2_
  22.3 0.1 collective-permute-start.5
  22.4 0.0 collective-permute-done.2.refs_3_
  22.4 2.0 %collective-permute-start.7 = (bf16[256,256]{1,0:T(8,128)(2,1)S(1)}, bf16[256,256]{1,0:T(8,128)(2,1)S(1)}, u32[]{:S(2)}, u32[]{:S(2)}) collective-permute-start(bf16[256,256]{1,0:T(8,128)(2,1)S(1)} %collective-permute-done.2.refs_3_), channel_id=1, source_target_pairs={{0,4},{2,6},{4,0},{6,2},{8,12},{10,14},{12,8},{14,10},{1,5},{3,7},... | collective-permute-start | bytes 393224 | tf_op jit(solution)/shard_map/ppermute | solution.py:169
  24.4 0.0 collective-permute-done.3.refs_4_
  24.4 0.0 collective-permute-done.4.refs_5_
  24.4 3.5 %shard_map.39 = (bf16[4096,256]{1,0:T(8,128)(2,1)S(1)}, f32[1,256]{1,0:T(1,128)S(1)}) custom-call(s32[16,256]{1,0:T(8,128)S(1)} %bitcast.8, f32[1,256]{1,0:T(1,128)S(1)} %shard_map.38.some_ref, bf16[256,256]{1,0:T(8,128)(2,1)S(1)} %get-tuple-element.15.a_ref.refs_0_, bf16[256,256]{1,0:T(8,128)(2,1)S(1)} %collective-permute-done.b_ref.refs_1_, ...), custom_call_target="tpu_custom_call" | custom-call | flops 3221225472 | bytes 803840 | tf_op jit(solution)/shard_map/pallas_call | solution.py:18
  28.0 0.8 %collective-permute-done.5.chunk_ref = bf16[256,256]{1,0:T(8,128)(2,1)S(1)} collective-permute-done((bf16[256,256]{1,0:T(8,128)(2,1)S(1)}, bf16[256,256]{1,0:T(8,128)(2,1)S(1)}, u32[]{:S(2)}, u32[]{:S(2)}) %collective-permute-start.5) | collective-permute-done | bytes 131104 | tf_op jit(solution)/shard_map/ppermute | solution.py:169
  28.7 1.3 %shard_map.40 = (bf16[4096,256]{1,0:T(8,128)(2,1)S(1)}, f32[1,256]{1,0:T(1,128)S(1)}) custom-call(s32[16,256]{1,0:T(8,128)S(1)} %bitcast.9, bf16[4096,256]{1,0:T(8,128)(2,1)S(1)} %get-tuple-element.17.moved_ref, f32[1,256]{1,0:T(1,128)S(1)} %get-tuple-element.18.squares_ref, bf16[256,256]{1,0:T(8,128)(2,1)S(1)} %collective-permute-done.5.chunk_ref), custom_call_target="tpu_custom_call" | custom-call | flops 536870912 | bytes 2245632 | tf_op jit(solution)/shard_map/pallas_call | solution.py:18
  30.1 0.6 %collective-permute-done.7.last_ref = bf16[256,256]{1,0:T(8,128)(2,1)S(1)} collective-permute-done((bf16[256,256]{1,0:T(8,128)(2,1)S(1)}, bf16[256,256]{1,0:T(8,128)(2,1)S(1)}, u32[]{:S(2)}, u32[]{:S(2)}) %collective-permute-start.7) | collective-permute-done | bytes 131104 | tf_op jit(solution)/shard_map/ppermute | solution.py:169
  30.7 0.0 collective-permute-done.6.sib_ref
  30.7 2.4 %shard_map.41 = f32[16,8,128]{2,1,0:T(8,128)S(1)} custom-call(s32[16,256]{1,0:T(8,128)S(1)} %bitcast.10, bf16[4096,256]{1,0:T(8,128)(2,1)S(1)} %get-tuple-element.19.moved_ref, f32[1,256]{1,0:T(1,128)S(1)} %get-tuple-element.20.squares_ref, bf16[256,2048]{1,0:T(8,128)(2,1)S(1)} %get-tuple-element.21.own_ref, ...), custom_call_target="tpu_custom_call" | custom-call | flops 1610612736 | bytes 4342784 | tf_op jit(solution)/shard_map/pallas_call | solution.py:18
  33.2 10.4 %all_to_all.17 = f32[16,8,128]{2,1,0:T(8,128)S(1)} all-to-all(f32[16,8,128]{2,1,0:T(8,128)S(1)} %shard_map.41), channel_id=1, replica_groups=mesh['perm'=2,'subj'=8,'vert'=2] {'perm','subj'}, dimensions={0} | all-to-all | bytes 131072 | tf_op jit(solution)/shard_map/all_to_all | solution.py:233
  43.6 0.6 %div.12 = f32[1024]{0:T(1024)} divide(f32[1024]{0:T(1024)S(1)} %bitcast.14, f32[1024]{0:T(1024)S(1)} %bitcast.15) | non-fusion elementwise | flops 1024 | bytes 12288 | tf_op jit(solution)/shard_map/div | solution.py:239
  (5 shorter events, 0.1 us)
Async XLA Ops:
  1.6 29.1 %collective-permute-start.6 = (bf16[256,2048]{1,0:T(8,128)(2,1)S(1)}, bf16[256,2048]{1,0:T(8,128)(2,1)S(1)}, u32[]{:S(2)}, u32[]{:S(2)}) collective-permute-start(bf16[256,2048]{1,0:T(8,128)(2,1)S(1)} %get-tuple-element.22), channel_id=1, source_target_pairs={{0,2},{2,0},{4,6},{6,4},{8,10},{10,8},{12,14},{14,12},{1,3},{3,1},... | collective-permute-start | bytes 3145736 | tf_op jit(solution)/shard_map/ppermute | solution.py:169
  2.1 4.1 %collective-permute-start = (bf16[256,256]{1,0:T(8,128)(2,1)S(1)}, bf16[256,256]{1,0:T(8,128)(2,1)S(1)}, u32[]{:S(2)}, u32[]{:S(2)}) collective-permute-start(bf16[256,256]{1,0:T(8,128)(2,1)S(1)} %get-tuple-element.16), channel_id=1, source_target_pairs={{0,2},{2,0},{4,6},{6,4},{8,10},{10,8},{12,14},{14,12},{1,3},{3,1},... | collective-permute-start | bytes 393224 | tf_op jit(solution)/shard_map/ppermute | solution.py:169
  2.2 20.1 %collective-permute-start.1 = (bf16[256,256]{1,0:T(8,128)(2,1)S(1)}, bf16[256,256]{1,0:T(8,128)(2,1)S(1)}, u32[]{:S(2)}, u32[]{:S(2)}) collective-permute-start(bf16[256,256]{1,0:T(8,128)(2,1)S(1)} %get-tuple-element.15.a_ref.refs_0_), channel_id=1, source_target_pairs={{0,8},{2,10},{4,12},{6,14},{8,0},{10,2},{12,4},{14,6},{1,9},{3,11}... | collective-permute-start | bytes 393224 | tf_op jit(solution)/shard_map/ppermute | solution.py:169
  6.2 16.2 %collective-permute-start.2 = (bf16[256,256]{1,0:T(8,128)(2,1)S(1)}, bf16[256,256]{1,0:T(8,128)(2,1)S(1)}, u32[]{:S(2)}, u32[]{:S(2)}) collective-permute-start(bf16[256,256]{1,0:T(8,128)(2,1)S(1)} %collective-permute-done.b_ref.refs_1_), channel_id=1, source_target_pairs={{0,8},{2,10},{4,12},{6,14},{8,0},{10,2},{12,4},{14,6},{1,9},{3,11}... | collective-permute-start | bytes 393224 | tf_op jit(solution)/shard_map/ppermute | solution.py:169
  8.5 15.9 %collective-permute-start.3 = (bf16[256,256]{1,0:T(8,128)(2,1)S(1)}, bf16[256,256]{1,0:T(8,128)(2,1)S(1)}, u32[]{:S(2)}, u32[]{:S(2)}) collective-permute-start(bf16[256,256]{1,0:T(8,128)(2,1)S(1)} %get-tuple-element.15.a_ref.refs_0_), channel_id=1, source_target_pairs={{0,4},{2,6},{4,0},{6,2},{8,12},{10,14},{12,8},{14,10},{1,5},{3,7},... | collective-permute-start | bytes 393224 | tf_op jit(solution)/shard_map/ppermute | solution.py:169
  10.1 14.3 %collective-permute-start.4 = (bf16[256,256]{1,0:T(8,128)(2,1)S(1)}, bf16[256,256]{1,0:T(8,128)(2,1)S(1)}, u32[]{:S(2)}, u32[]{:S(2)}) collective-permute-start(bf16[256,256]{1,0:T(8,128)(2,1)S(1)} %collective-permute-done.b_ref.refs_1_), channel_id=1, source_target_pairs={{0,4},{2,6},{4,0},{6,2},{8,12},{10,14},{12,8},{14,10},{1,5},{3,7},... | collective-permute-start | bytes 393224 | tf_op jit(solution)/shard_map/ppermute | solution.py:169
  22.3 6.4 %collective-permute-start.5 = (bf16[256,256]{1,0:T(8,128)(2,1)S(1)}, bf16[256,256]{1,0:T(8,128)(2,1)S(1)}, u32[]{:S(2)}, u32[]{:S(2)}) collective-permute-start(bf16[256,256]{1,0:T(8,128)(2,1)S(1)} %collective-permute-done.1.refs_2_), channel_id=1, source_target_pairs={{0,4},{2,6},{4,0},{6,2},{8,12},{10,14},{12,8},{14,10},{1,5},{3,7},... | collective-permute-start | bytes 393224 | tf_op jit(solution)/shard_map/ppermute | solution.py:169
  22.4 8.3 %collective-permute-start.7 = (bf16[256,256]{1,0:T(8,128)(2,1)S(1)}, bf16[256,256]{1,0:T(8,128)(2,1)S(1)}, u32[]{:S(2)}, u32[]{:S(2)}) collective-permute-start(bf16[256,256]{1,0:T(8,128)(2,1)S(1)} %collective-permute-done.2.refs_3_), channel_id=1, source_target_pairs={{0,4},{2,6},{4,0},{6,2},{8,12},{10,14},{12,8},{14,10},{1,5},{3,7},... | collective-permute-start | bytes 393224 | tf_op jit(solution)/shard_map/ppermute | solution.py:169

commit v3 on v2

v3 whole, which is shorter than its diff:
```python
import functools

import jax
import jax.numpy as jnp
from jax import lax
from jax.experimental import pallas as pl
from jax.experimental.pallas import tpu as pltpu
from jax.sharding import PartitionSpec as P

BF16, F32, I32 = jnp.bfloat16, jnp.float32, jnp.int32
LANES = 128


def after(x, *others):
    return lax.optimization_barrier((x, *others))[0]


def call(body, out, *args, flops=0, scratch=(), from_hbm=0, to_hbm=0):
    ins = [pltpu.HBM if i < from_hbm else pltpu.VMEM for i in range(len(args))]
    outs = [pltpu.HBM if i < to_hbm else pltpu.VMEM for i in range(len(out))]
    size = sum(a.size * a.dtype.itemsize for a in args)
    return pl.pallas_call(
        body,
        out_shape=[space(shape, dtype) for space, (shape, dtype) in zip(outs, out)],
        in_specs=[pl.BlockSpec(memory_space=space) for space in ins],
        out_specs=[pl.BlockSpec(memory_space=space) for space in outs],
        scratch_shapes=scratch,
        compiler_params=pltpu.CompilerParams(vmem_limit_bytes=24 << 20),
        cost_estimate=pl.CostEstimate(
            flops=flops, bytes_accessed=size, transcendentals=0
        ),
    )(*[pltpu.with_memory_space_constraint(a, s) for a, s in zip(args, ins)])


def dot(a, b):
    return jnp.dot(a, b, preferred_element_type=F32)


def tile_of(index, rows):
    return pl.ds(pl.multiple_of(index * rows, LANES), rows)


def square_rows(ref):
    v = ref[...].astype(F32)
    return jnp.sum(v * v, axis=0, keepdims=True)


def cut(phen_ref, shuffle_ref, everyone_ref, mine_ref, others_ref, line_ref, lines_ref, sems):
    width = mine_ref.shape[1]
    core, first = lax.rem(lax.axis_index("subj"), 2), lax.axis_index("perm") * 2
    copies = [
        pltpu.make_async_copy(shuffle_ref, line_ref, sems.at[0]),
        pltpu.make_async_copy(
            phen_ref.at[:, tile_of(first + core, width)], mine_ref, sems.at[1]
        ),
        pltpu.make_async_copy(
            phen_ref.at[:, tile_of(first + 1 - core, width)], others_ref, sems.at[2]
        ),
    ]
    for copy in copies:
        copy.start()
    copies[0].wait()
    for h in range(line_ref.shape[1] // LANES):
        piece = line_ref[:, h * LANES : (h + 1) * LANES]
        lines_ref[:, h, :] = jnp.broadcast_to(piece, (lines_ref.shape[0], LANES))
    send = pltpu.make_async_copy(lines_ref, everyone_ref, sems.at[3])
    send.start()
    for copy in copies[1:]:
        copy.wait()
    send.wait()


def clear(order, kin_ref, own_ref, *refs):
    sib_refs, (all_ref, sem) = refs[:-2], refs[-2:]
    rows, me = kin_ref.shape[0], lax.axis_index("subj")
    copy = pltpu.make_async_copy(kin_ref, all_ref, sem)
    copy.start()
    copy.wait()
    r = lax.broadcasted_iota(I32, (rows, rows), 0)
    c = lax.broadcasted_iota(I32, (rows, rows), 1)
    for i, source in enumerate(order):
        block = all_ref[:, tile_of(me ^ source, rows)]
        if source == 0:
            block = jnp.where(r == c, 0.0, block.astype(F32)).astype(BF16)
        own_ref[:, i * rows : (i + 1) * rows] = block
        at = order.index(source ^ 1) * rows
        for sib_ref in sib_refs:
            if 0 <= at < sib_ref.shape[1]:
                sib_ref[:, at : at + rows] = block
            at -= sib_ref.shape[1]


def columns_of(shuffle_ref, perm, subj, perms, rows):
    lines = shuffle_ref[perm * (shuffle_ref.shape[0] // perms) + subj]
    column = jnp.concatenate(
        [
            jnp.transpose(jnp.broadcast_to(lines[h : h + 1], (LANES, LANES)))
            for h in range(rows // LANES)
        ],
        axis=0,
    )
    high = lax.div(column, rows)
    low = column - high * rows
    return high.astype(F32).astype(BF16), low.astype(F32).astype(BF16)


def picker(digits, block, rows):
    high, low = digits
    shape = high.shape
    lane = lax.broadcasted_iota(I32, shape, 1)
    one, zero = jnp.ones(shape, BF16), jnp.zeros(shape, BF16)
    number = jnp.full(shape, block, F32).astype(BF16)
    inside = jnp.where(high == number, low, jnp.full(shape, -1, BF16))
    tiles = [
        jnp.where(inside == (lane + t).astype(F32).astype(BF16), one, zero)
        for t in range(0, rows, LANES)
    ]
    return jnp.concatenate(tiles, axis=1)


def find(order, chunks, digits, rows):
    me = lax.axis_index("subj")
    parts = [dot(picker(digits, me ^ s, rows), c[...]) for s, c in zip(order, chunks)]
    return sum(parts).astype(BF16)


def tile(index, rows):
    return slice(index * rows, (index + 1) * rows)


def times(parts, x):
    total, at = 0.0, 0
    for part in parts:
        total += dot(part[...], x[at : at + part.shape[1], :])
        at += part.shape[1]
    return total


def square(a_ref, b_ref, out_ref):
    out_ref[...] = square_rows(a_ref) + square_rows(b_ref)


def move(order, perms, shuffle_ref, some_ref, *refs):
    chunks, (moved_ref, squares_ref) = refs[:-2], refs[-2:]
    rows, me = chunks[0].shape[0], lax.axis_index("subj")
    n = len(order)
    for p in range(perms):
        for i in range(n):
            digits = columns_of(shuffle_ref, p, me ^ order[i], perms, rows)
            moved_ref[tile(p * n + i, rows), :] = find(order, chunks, digits, rows)
    squares_ref[...] = some_ref[...] + sum(square_rows(c) for c in chunks[2:])


def finish(order, perms, shuffle_ref, moved_ref, squares_ref, own_ref, last_ref, *refs):
    sib_refs, (out_ref, full_ref) = refs[:-2], refs[-2:]
    rows, me = last_ref.shape[0], lax.axis_index("subj")
    n = len(order)
    squares = squares_ref[...] + square_rows(last_ref)
    halves = squares.shape[1] // LANES
    dests = out_ref.shape[0] // perms
    for p in range(perms):
        for i in range(n):
            digits = columns_of(shuffle_ref, p, me ^ order[i], perms, rows)
            found = find(order[-1:], [last_ref], digits, rows)
            full_ref[tile(i, rows), :] = moved_ref[tile(p * n + i, rows), :] + found
        cross = jnp.zeros_like(squares)
        for g, product in enumerate([dot(own_ref[...], full_ref[...]), times(sib_refs, full_ref)]):
            mine = full_ref[tile(g, rows), :].astype(F32)
            cross += jnp.sum(mine * product, axis=0, keepdims=True)
        lines = [cross[:, h * LANES : (h + 1) * LANES] for h in range(halves)]
        lines += [squares[:, h * LANES : (h + 1) * LANES] for h in range(halves)]
        lines += [jnp.zeros((8 - 2 * halves, LANES), F32)]
        block = jnp.concatenate(lines, axis=0)
        for d in range(dests):
            out_ref[p * dests + d] = block


def per_device(n_perm, n_subj, kinship, phenotype, shuffle):
    rows, subjects = kinship.shape
    width = phenotype.shape[1] // (2 * n_perm)

    def exchange(x, mask):
        return lax.ppermute(x, "subj", [(i, i ^ mask) for i in range(n_subj)])

    order, step = [0, 1], n_subj // 2
    while step > 1:
        order = order + [s ^ step for s in order]
        step //= 2

    parts = [k * subjects // 8 for k in (3,3,2)]
    everyone, mine, others = call(
        cut,
        [
            ((n_perm * n_subj, 8, LANES), I32),
            ((rows, width), BF16),
            ((rows, width), BF16),
        ],
        phenotype,
        shuffle[None],
        from_hbm=2,
        to_hbm=1,
        scratch=[
            pltpu.VMEM((1, rows), I32),
            pltpu.VMEM((n_perm * n_subj, 8, LANES), I32),
            pltpu.SemaphoreType.DMA((4,)),
        ],
    )
    own_kin, *for_sib = call(
        functools.partial(clear, order),
        [((rows, subjects), BF16)] + [((rows, part), BF16) for part in parts],
        kinship,
        from_hbm=1,
        scratch=[pltpu.VMEM((rows, subjects), BF16), pltpu.SemaphoreType.DMA],
        flops=0,
    )
    received = exchange(others, 1)
    shuffles = lax.all_to_all(everyone, ("perm", "subj"), 0, 0, tiled=True)
    sib_kin = [
        exchange(x if k < 0 else after(x, shuffles), 1) for k, x in enumerate(for_sib)
    ]

    chunks, step = [mine, received], n_subj // 2
    while step > 1:
        chunks = chunks + [exchange(x, step) for x in chunks]
        step //= 2

    table = [((n_perm * subjects, width), BF16), ((1, width), F32)]
    unit = 2 * rows * rows * width
    tiles = n_perm * n_subj
    squares = call(square, [((1, width), F32)], mine, received)[0]
    moved, squares = call(
        functools.partial(move, order, n_perm),
        table,
        shuffles,
        squares,
        *chunks[:-1],
        flops=unit * tiles * (n_subj - 1),
    )
    sums = call(
        functools.partial(finish, order, n_perm),
        [((tiles, 8, LANES), F32)],
        shuffles,
        moved,
        squares,
        own_kin,
        chunks[-1],
        *sib_kin,
        flops=unit * tiles * 3,
        scratch=[pltpu.VMEM((subjects, width), BF16)],
    )[0]
    sums = lax.all_to_all(sums, ("perm", "subj"), 0, 0, tiled=True)
    sums = sums.reshape(n_perm, n_subj // 2, 2, 8, LANES)
    lines = width // LANES
    cross = jnp.sum(sums[:, :, :, :lines], axis=1)
    squares = sums[:, 0, :, lines : 2 * lines]
    count = jnp.float32(subjects)
    result = cross / (jnp.sqrt(count) * (squares / subjects + 1e-05))
    return result.reshape(-1)


def solution(mesh):
    in_specs = (P("subj", None), P("subj", "vert"), P(("perm", "subj")))
    out_specs = P(("perm", "vert"))
    body = functools.partial(per_device, mesh.shape["perm"], mesh.shape["subj"])
    return jax.shard_map(
        body, mesh=mesh, in_specs=in_specs, out_specs=out_specs, check_vma=False
    )
```

time: 44.4 us -> 42.4 us (0.955)
  blocking collectives: 22.1 us -> 11.8 us
  starting transfers between devices: 11 us -> 16.9 us
  waiting for transfers between devices: 1.42 us -> 3.39 us
    all_to_all x1 -> x0, blocking collectives: 11.7 us -> none  [per_device(): shuffles = lax.all_to_all(everyone, ('perm', 'subj'), 0, 0, tiled=True)]
    all_to_all x0 -> x1, starting transfers between devices: none -> 3.49 us  [per_device(): shuffles = lax.all_to_all(everyone, ('perm', 'subj'), 0, 0, tiled=True)]
    ppermute x8 -> x10, starting transfers between devices: 11 us -> 13.5 us  [exchange(): return lax.ppermute(x, 'subj', [(i, i ^ mask) for i in range(n_subj)])]
    all_to_all x1, blocking collectives: 10.4 us -> 11.8 us  [per_device(): sums = lax.all_to_all(sums, ('perm', 'subj'), 0, 0, tiled=True)]
    all_to_all x0 -> x1, waiting for transfers between devices: none -> 1.1 us  [per_device(): shuffles = lax.all_to_all(everyone, ('perm', 'subj'), 0, 0, tiled=True)]
    ppermute x8 -> x10, waiting for transfers between devices: 1.42 us -> 2.29 us  [exchange(): return lax.ppermute(x, 'subj', [(i, i ^ mask) for i in range(n_subj)])]
  transfers between devices with their start and end apart: 8 -> 11, of which waited for: 2 -> 2; matrix products, arithmetic and copies ran while one was open for 0% -> 0% of each run, Pallas kernels for 11% -> 13%
where the time goes in v3:
time: 42.4 us; the launch traced here: 42.1 us
  starting transfers between devices  16.9 us (40%)
  blocking collectives  11.8 us (28%)
  Pallas kernels  9.22 us (22%)
  waiting for transfers between devices  3.39 us (8%)
  other arithmetic  0.62 us (1%)
    ppermute x10, starting transfers between devices, exchange(): return lax.ppermute(x, 'subj', [(i, i ^ mask) for i in range(n_subj)])  13.5 us
    all_to_all x1, blocking collectives, per_device(): sums = lax.all_to_all(sums, ('perm', 'subj'), 0, 0, tiled=True)  11.8 us
    pallas_call x5, Pallas kernels, call(): pl.pallas_call(body, out_shape=[space(shape, dtype) for space, (shape, dt...  9.22 us
    all_to_all x1, starting transfers between devices, per_device(): shuffles = lax.all_to_all(everyone, ('perm', 'subj'), 0, 0, tiled=True)  3.49 us
    ppermute x10, waiting for transfers between devices, exchange(): return lax.ppermute(x, 'subj', [(i, i ^ mask) for i in range(n_subj)])  2.29 us
    all_to_all x1, waiting for transfers between devices, per_device(): shuffles = lax.all_to_all(everyone, ('perm', 'subj'), 0, 0, tiled=True)  1.1 us
  transfers between devices with their start and end apart: 11, of which 2 were waited for; matrix products, arithmetic and copies ran while one was open for 0% of the time, Pallas kernels for 13%

profile of v3, /device:TPU:0, one launch (start us, length us, event | category | flops | bytes accessed | tf_op | source)
XLA Modules:
  0.0 42.1 jit_solution(16640056554544250328)
XLA Ops:
  0.0 1.4 %shard_map.37 = (s32[16,8,128]{2,1,0:T(8,128)}, bf16[256,256]{1,0:T(8,128)(2,1)S(1)}, bf16[256,256]{1,0:T(8,128)(2,1)S(1)}) custom-call(bf16[256,1024]{1,0:T(8,128)(2,1)} %phen_ref.1, s32[1,256]{1,0:T(1,128)} %bitcast.8), custom_call_target="tpu_custom_call" | custom-call | bytes 525312 | tf_op jit(solution)/shard_map/pallas_call | solution.py:22
  1.4 0.5 %collective-permute-start = (bf16[256,256]{1,0:T(8,128)(2,1)S(1)}, bf16[256,256]{1,0:T(8,128)(2,1)S(1)}, u32[]{:S(2)}, u32[]{:S(2)}) collective-permute-start(bf16[256,256]{1,0:T(8,128)(2,1)S(1)} %get-tuple-element.19), channel_id=1, source_target_pairs={{0,2},{2,0},{4,6},{6,4},{8,10},{10,8},{12,14},{14,12},{1,3},{3,1},... | collective-permute-start | bytes 393224 | tf_op jit(solution)/shard_map/ppermute | solution.py:183
  1.9 3.7 %collective-permute-start.1 = (bf16[256,256]{1,0:T(8,128)(2,1)S(1)}, bf16[256,256]{1,0:T(8,128)(2,1)S(1)}, u32[]{:S(2)}, u32[]{:S(2)}) collective-permute-start(bf16[256,256]{1,0:T(8,128)(2,1)S(1)} %get-tuple-element.18.a_ref.refs_0_), channel_id=1, source_target_pairs={{0,8},{2,10},{4,12},{6,14},{8,0},{10,2},{12,4},{14,6},{1,9},{3,11}... | collective-permute-start | bytes 393224 | tf_op jit(solution)/shard_map/ppermute | solution.py:183
  5.5 1.6 %collective-permute-start.3 = (bf16[256,256]{1,0:T(8,128)(2,1)S(1)}, bf16[256,256]{1,0:T(8,128)(2,1)S(1)}, u32[]{:S(2)}, u32[]{:S(2)}) collective-permute-start(bf16[256,256]{1,0:T(8,128)(2,1)S(1)} %get-tuple-element.18.a_ref.refs_0_), channel_id=1, source_target_pairs={{0,4},{2,6},{4,0},{6,2},{8,12},{10,14},{12,8},{14,10},{1,5},{3,7},... | collective-permute-start | bytes 393224 | tf_op jit(solution)/shard_map/ppermute | solution.py:183
  7.1 3.5 %all-to-all-start = ((s32[16,8,128]{2,1,0:T(8,128)}), s32[16,8,128]{2,1,0:T(8,128)S(1)}, u32[]{:S(2)}, u32[]{:S(2)}) async-start(s32[16,8,128]{2,1,0:T(8,128)} %get-tuple-element.17), calls=%async_computation | async-start | bytes 131072 | tf_op jit(solution)/shard_map/all_to_all | solution.py:217
  10.6 0.0 collective-permute-done.b_ref.refs_1_
  10.6 1.9 %collective-permute-start.4 = (bf16[256,256]{1,0:T(8,128)(2,1)S(1)}, bf16[256,256]{1,0:T(8,128)(2,1)S(1)}, u32[]{:S(2)}, u32[]{:S(2)}) collective-permute-start(bf16[256,256]{1,0:T(8,128)(2,1)S(1)} %collective-permute-done.b_ref.refs_1_), channel_id=1, source_target_pairs={{0,4},{2,6},{4,0},{6,2},{8,12},{10,14},{12,8},{14,10},{1,5},{3,7},... | collective-permute-start | bytes 393224 | tf_op jit(solution)/shard_map/ppermute | solution.py:183
  12.5 2.4 %collective-permute-start.2 = (bf16[256,256]{1,0:T(8,128)(2,1)S(1)}, bf16[256,256]{1,0:T(8,128)(2,1)S(1)}, u32[]{:S(2)}, u32[]{:S(2)}) collective-permute-start(bf16[256,256]{1,0:T(8,128)(2,1)S(1)} %collective-permute-done.b_ref.refs_1_), channel_id=1, source_target_pairs={{0,8},{2,10},{4,12},{6,14},{8,0},{10,2},{12,4},{14,6},{1,9},{3,11}... | collective-permute-start | bytes 393224 | tf_op jit(solution)/shard_map/ppermute | solution.py:183
  14.9 0.0 collective-permute-done.1.refs_2_
  14.9 0.6 %collective-permute-start.5 = (bf16[256,256]{1,0:T(8,128)(2,1)S(1)}, bf16[256,256]{1,0:T(8,128)(2,1)S(1)}, u32[]{:S(2)}, u32[]{:S(2)}) collective-permute-start(bf16[256,256]{1,0:T(8,128)(2,1)S(1)} %collective-permute-done.1.refs_2_), channel_id=1, source_target_pairs={{0,4},{2,6},{4,0},{6,2},{8,12},{10,14},{12,8},{14,10},{1,5},{3,7},... | collective-permute-start | bytes 393224 | tf_op jit(solution)/shard_map/ppermute | solution.py:183
  15.4 1.4 %shard_map.40 = (bf16[256,2048]{1,0:T(8,128)(2,1)S(1)}, bf16[256,768]{1,0:T(8,128)(2,1)S(1)}, bf16[256,768]{1,0:T(8,128)(2,1)S(1)}, bf16[256,512]{1,0:T(8,128)(2,1)S(1)}) custom-call(bf16[256,2048]{1,0:T(8,128)(2,1)} %kin_ref.1), custom_call_target="tpu_custom_call" | custom-call | bytes 1048576 | tf_op jit(solution)/shard_map/pallas_call | solution.py:22
  16.9 1.1 %all-to-all-done.shuffle_ref = s32[16,8,128]{2,1,0:T(8,128)S(1)} async-done(((s32[16,8,128]{2,1,0:T(8,128)}), s32[16,8,128]{2,1,0:T(8,128)S(1)}, u32[]{:S(2)}, u32[]{:S(2)}) %all-to-all-start) | async-done | bytes 65568 | tf_op jit(solution)/shard_map/all_to_all | solution.py:217
  18.0 0.0 collective-permute-start.8
  18.0 0.0 collective-permute-done.3.refs_4_
  18.0 0.5 %collective-permute-start.7 = (bf16[256,768]{1,0:T(8,128)(2,1)S(1)}, bf16[256,768]{1,0:T(8,128)(2,1)S(1)}, u32[]{:S(2)}, u32[]{:S(2)}) collective-permute-start(bf16[256,768]{1,0:T(8,128)(2,1)S(1)} %get-tuple-element.24), channel_id=1, source_target_pairs={{0,2},{2,0},{4,6},{6,4},{8,10},{10,8},{12,14},{14,12},{1,3},{3,1},... | collective-permute-start | bytes 1179656 | tf_op jit(solution)/shard_map/ppermute | solution.py:183
  18.5 2.3 %collective-permute-done.4.refs_5_ = bf16[256,256]{1,0:T(8,128)(2,1)S(1)} collective-permute-done((bf16[256,256]{1,0:T(8,128)(2,1)S(1)}, bf16[256,256]{1,0:T(8,128)(2,1)S(1)}, u32[]{:S(2)}, u32[]{:S(2)}) %collective-permute-start.4) | collective-permute-done | bytes 131104 | tf_op jit(solution)/shard_map/ppermute | solution.py:183
  20.8 0.0 collective-permute-start.9
  20.8 0.0 collective-permute-done.2.refs_3_
  20.8 2.4 %collective-permute-start.6 = (bf16[256,256]{1,0:T(8,128)(2,1)S(1)}, bf16[256,256]{1,0:T(8,128)(2,1)S(1)}, u32[]{:S(2)}, u32[]{:S(2)}) collective-permute-start(bf16[256,256]{1,0:T(8,128)(2,1)S(1)} %collective-permute-done.2.refs_3_), channel_id=1, source_target_pairs={{0,4},{2,6},{4,0},{6,2},{8,12},{10,14},{12,8},{14,10},{1,5},{3,7},... | collective-permute-start | bytes 393224 | tf_op jit(solution)/shard_map/ppermute | solution.py:183
  23.2 0.0 collective-permute-done.5.refs_6_
  23.2 4.0 %shard_map.39 = (bf16[4096,256]{1,0:T(8,128)(2,1)S(1)}, f32[1,256]{1,0:T(1,128)S(1)}) custom-call(s32[16,8,128]{2,1,0:T(8,128)S(1)} %all-to-all-done.shuffle_ref, f32[1,256]{1,0:T(1,128)S(1)} %shard_map.38.some_ref, bf16[256,256]{1,0:T(8,128)(2,1)S(1)} %get-tuple-element.18.a_ref.refs_0_, bf16[256,256]{1,0:T(8,128)(2,1)S(1)} %collective-permute-done.b_ref.refs_1_, ...), custom_call_target="tpu_custom_call" | custom-call | flops 3758096384 | bytes 984064 | tf_op jit(solution)/shard_map/pallas_call | solution.py:22
  27.2 0.0 collective-permute-done.9.refs_2_
  27.2 0.0 collective-permute-done.6.last_ref
  27.2 0.0 collective-permute-done.8.refs_1_
  27.3 0.0 collective-permute-done.7.refs_0_
  27.3 2.4 %shard_map.41 = f32[16,8,128]{2,1,0:T(8,128)S(1)} custom-call(s32[16,8,128]{2,1,0:T(8,128)S(1)} %all-to-all-done.shuffle_ref, bf16[4096,256]{1,0:T(8,128)(2,1)S(1)} %get-tuple-element.20.moved_ref, f32[1,256]{1,0:T(1,128)S(1)} %get-tuple-element.21.squares_ref, bf16[256,2048]{1,0:T(8,128)(2,1)S(1)} %get-tuple-element.22.own_ref, ...), custom_call_target="tpu_custom_call" | custom-call | flops 1610612736 | bytes 4391936 | tf_op jit(solution)/shard_map/pallas_call | solution.py:22
  29.6 11.8 %all_to_all.10 = f32[16,8,128]{2,1,0:T(8,128)S(1)} all-to-all(f32[16,8,128]{2,1,0:T(8,128)S(1)} %shard_map.41), channel_id=1, replica_groups=mesh['perm'=2,'subj'=8,'vert'=2] {'perm','subj'}, dimensions={0} | all-to-all | bytes 131072 | tf_op jit(solution)/shard_map/all_to_all | solution.py:251
  41.5 0.6 %div.12 = f32[1024]{0:T(1024)} divide(f32[1024]{0:T(1024)S(1)} %bitcast.6, f32[1024]{0:T(1024)S(1)} %bitcast.7) | non-fusion elementwise | flops 1024 | bytes 12288 | tf_op jit(solution)/shard_map/div | solution.py:257
  (3 shorter events, 0.1 us)
Async XLA Ops:
  1.4 9.3 %collective-permute-start = (bf16[256,256]{1,0:T(8,128)(2,1)S(1)}, bf16[256,256]{1,0:T(8,128)(2,1)S(1)}, u32[]{:S(2)}, u32[]{:S(2)}) collective-permute-start(bf16[256,256]{1,0:T(8,128)(2,1)S(1)} %get-tuple-element.19), channel_id=1, source_target_pairs={{0,2},{2,0},{4,6},{6,4},{8,10},{10,8},{12,14},{14,12},{1,3},{3,1},... | collective-permute-start | bytes 393224 | tf_op jit(solution)/shard_map/ppermute | solution.py:183
  1.9 13.0 %collective-permute-start.1 = (bf16[256,256]{1,0:T(8,128)(2,1)S(1)}, bf16[256,256]{1,0:T(8,128)(2,1)S(1)}, u32[]{:S(2)}, u32[]{:S(2)}) collective-permute-start(bf16[256,256]{1,0:T(8,128)(2,1)S(1)} %get-tuple-element.18.a_ref.refs_0_), channel_id=1, source_target_pairs={{0,8},{2,10},{4,12},{6,14},{8,0},{10,2},{12,4},{14,6},{1,9},{3,11}... | collective-permute-start | bytes 393224 | tf_op jit(solution)/shard_map/ppermute | solution.py:183
  5.5 12.4 %collective-permute-start.3 = (bf16[256,256]{1,0:T(8,128)(2,1)S(1)}, bf16[256,256]{1,0:T(8,128)(2,1)S(1)}, u32[]{:S(2)}, u32[]{:S(2)}) collective-permute-start(bf16[256,256]{1,0:T(8,128)(2,1)S(1)} %get-tuple-element.18.a_ref.refs_0_), channel_id=1, source_target_pairs={{0,4},{2,6},{4,0},{6,2},{8,12},{10,14},{12,8},{14,10},{1,5},{3,7},... | collective-permute-start | bytes 393224 | tf_op jit(solution)/shard_map/ppermute | solution.py:183
  7.1 10.8 %all-to-all-start = ((s32[16,8,128]{2,1,0:T(8,128)}), s32[16,8,128]{2,1,0:T(8,128)S(1)}, u32[]{:S(2)}, u32[]{:S(2)}) async-start(s32[16,8,128]{2,1,0:T(8,128)} %get-tuple-element.17), calls=%async_computation | async-start | bytes 131072 | tf_op jit(solution)/shard_map/all_to_all | solution.py:217
  10.6 10.1 %collective-permute-start.4 = (bf16[256,256]{1,0:T(8,128)(2,1)S(1)}, bf16[256,256]{1,0:T(8,128)(2,1)S(1)}, u32[]{:S(2)}, u32[]{:S(2)}) collective-permute-start(bf16[256,256]{1,0:T(8,128)(2,1)S(1)} %collective-permute-done.b_ref.refs_1_), channel_id=1, source_target_pairs={{0,4},{2,6},{4,0},{6,2},{8,12},{10,14},{12,8},{14,10},{1,5},{3,7},... | collective-permute-start | bytes 393224 | tf_op jit(solution)/shard_map/ppermute | solution.py:183
  12.5 8.3 %collective-permute-start.2 = (bf16[256,256]{1,0:T(8,128)(2,1)S(1)}, bf16[256,256]{1,0:T(8,128)(2,1)S(1)}, u32[]{:S(2)}, u32[]{:S(2)}) collective-permute-start(bf16[256,256]{1,0:T(8,128)(2,1)S(1)} %collective-permute-done.b_ref.refs_1_), channel_id=1, source_target_pairs={{0,8},{2,10},{4,12},{6,14},{8,0},{10,2},{12,4},{14,6},{1,9},{3,11}... | collective-permute-start | bytes 393224 | tf_op jit(solution)/shard_map/ppermute | solution.py:183
  14.9 8.3 %collective-permute-start.5 = (bf16[256,256]{1,0:T(8,128)(2,1)S(1)}, bf16[256,256]{1,0:T(8,128)(2,1)S(1)}, u32[]{:S(2)}, u32[]{:S(2)}) collective-permute-start(bf16[256,256]{1,0:T(8,128)(2,1)S(1)} %collective-permute-done.1.refs_2_), channel_id=1, source_target_pairs={{0,4},{2,6},{4,0},{6,2},{8,12},{10,14},{12,8},{14,10},{1,5},{3,7},... | collective-permute-start | bytes 393224 | tf_op jit(solution)/shard_map/ppermute | solution.py:183
  18.0 9.3 %collective-permute-start.8 = (bf16[256,768]{1,0:T(8,128)(2,1)S(1)}, bf16[256,768]{1,0:T(8,128)(2,1)S(1)}, u32[]{:S(2)}, u32[]{:S(2)}) collective-permute-start(bf16[256,768]{1,0:T(8,128)(2,1)S(1)} %get-tuple-element.26), channel_id=1, source_target_pairs={{0,2},{2,0},{4,6},{6,4},{8,10},{10,8},{12,14},{14,12},{1,3},{3,1},... | collective-permute-start | bytes 1179656 | tf_op jit(solution)/shard_map/ppermute | solution.py:183
  18.0 9.3 %collective-permute-start.7 = (bf16[256,768]{1,0:T(8,128)(2,1)S(1)}, bf16[256,768]{1,0:T(8,128)(2,1)S(1)}, u32[]{:S(2)}, u32[]{:S(2)}) collective-permute-start(bf16[256,768]{1,0:T(8,128)(2,1)S(1)} %get-tuple-element.24), channel_id=1, source_target_pairs={{0,2},{2,0},{4,6},{6,4},{8,10},{10,8},{12,14},{14,12},{1,3},{3,1},... | collective-permute-start | bytes 1179656 | tf_op jit(solution)/shard_map/ppermute | solution.py:183
  20.8 6.5 %collective-permute-start.9 = (bf16[256,512]{1,0:T(8,128)(2,1)S(1)}, bf16[256,512]{1,0:T(8,128)(2,1)S(1)}, u32[]{:S(2)}, u32[]{:S(2)}) collective-permute-start(bf16[256,512]{1,0:T(8,128)(2,1)S(1)} %get-tuple-element.28), channel_id=1, source_target_pairs={{0,2},{2,0},{4,6},{6,4},{8,10},{10,8},{12,14},{14,12},{1,3},{3,1},... | collective-permute-start | bytes 786440 | tf_op jit(solution)/shard_map/ppermute | solution.py:183
  20.8 6.5 %collective-permute-start.6 = (bf16[256,256]{1,0:T(8,128)(2,1)S(1)}, bf16[256,256]{1,0:T(8,128)(2,1)S(1)}, u32[]{:S(2)}, u32[]{:S(2)}) collective-permute-start(bf16[256,256]{1,0:T(8,128)(2,1)S(1)} %collective-permute-done.2.refs_3_), channel_id=1, source_target_pairs={{0,4},{2,6},{4,0},{6,2},{8,12},{10,14},{12,8},{14,10},{1,5},{3,7},... | collective-permute-start | bytes 393224 | tf_op jit(solution)/shard_map/ppermute | solution.py:183

commit v4 on v3

--- a/solution.py
+++ b/solution.py
@@ -15,10 +15,11 @@
     return lax.optimization_barrier((x, *others))[0]
 
 
-def call(body, out, *args, flops=0, scratch=(), from_hbm=0, to_hbm=0):
+def call(body, out, *args, flops=0, scratch=(), from_hbm=0, to_hbm=0, size=None):
     ins = [pltpu.HBM if i < from_hbm else pltpu.VMEM for i in range(len(args))]
     outs = [pltpu.HBM if i < to_hbm else pltpu.VMEM for i in range(len(out))]
-    size = sum(a.size * a.dtype.itemsize for a in args)
+    if size is None:
+        size = sum(a.size * a.dtype.itemsize for a in args)
     return pl.pallas_call(
         body,
         out_shape=[space(shape, dtype) for space, (shape, dtype) in zip(outs, out)],
@@ -136,19 +137,18 @@
     return total
 
 
-def square(a_ref, b_ref, out_ref):
-    out_ref[...] = square_rows(a_ref) + square_rows(b_ref)
-
-
-def move(order, perms, shuffle_ref, some_ref, *refs):
-    chunks, (moved_ref, squares_ref) = refs[:-2], refs[-2:]
+def move(order, perms, sources, shuffle_ref, *refs):
+    n = len(order)
+    chunks, before, (moved_ref, squares_ref) = refs[: len(sources)], refs[len(sources) : -2], refs[-2:]
     rows, me = chunks[0].shape[0], lax.axis_index("subj")
-    n = len(order)
     for p in range(perms):
         for i in range(n):
             digits = columns_of(shuffle_ref, p, me ^ order[i], perms, rows)
-            moved_ref[tile(p * n + i, rows), :] = find(order, chunks, digits, rows)
-    squares_ref[...] = some_ref[...] + sum(square_rows(c) for c in chunks[2:])
+            here = tile(p * n + i, rows)
+            more = find(sources, chunks, digits, rows)
+            moved_ref[here, :] = before[0][here, :] + more if before else more
+    squares = sum(square_rows(c) for c in chunks)
+    squares_ref[...] = before[1][...] + squares if before else squares
 
 
 def finish(order, perms, shuffle_ref, moved_ref, squares_ref, own_ref, last_ref, *refs):
@@ -227,13 +227,23 @@
     table = [((n_perm * subjects, width), BF16), ((1, width), F32)]
     unit = 2 * rows * rows * width
     tiles = n_perm * n_subj
-    squares = call(square, [((1, width), F32)], mine, received)[0]
+    half = n_subj // 2
+    met = [0, 1, 2, half]
+    late = [i for i in range(n_subj - 1) if i not in met]
     moved, squares = call(
-        functools.partial(move, order, n_perm),
+        functools.partial(move, order, n_perm, [order[i] for i in met]),
         table,
         shuffles,
+        *[chunks[i] for i in met],
+        size=0,
+    )
+    moved, squares = call(
+        functools.partial(move, order, n_perm, [order[i] for i in late]),
+        table,
+        shuffles,
+        *[chunks[i] for i in late],
+        moved,
         squares,
-        *chunks[:-1],
         flops=unit * tiles * (n_subj - 1),
     )
     sums = call(

time: 42.4 us -> 41.3 us (0.974)
  blocking collectives: 11.8 us -> 11.1 us
  waiting for transfers between devices: 3.39 us -> 2.95 us
    all_to_all x1, blocking collectives: 11.8 us -> 11.1 us  [per_device(): sums = lax.all_to_all(sums, ('perm', 'subj'), 0, 0, tiled=True)]
    ppermute x10, waiting for transfers between devices: 2.29 us -> 1.85 us  [exchange(): return lax.ppermute(x, 'subj', [(i, i ^ mask) for i in range(n_subj)])]
  transfers between devices with their start and end apart: 11 -> 11, of which waited for: 2 -> 2; matrix products, arithmetic and copies ran while one was open for 0% -> 0% of each run, Pallas kernels for 13% -> 14%
where the time goes in v4:
time: 41.3 us; the launch traced here: 41 us
  starting transfers between devices  16.8 us (41%)
  blocking collectives  11.1 us (27%)
  Pallas kernels  9.46 us (23%)
  waiting for transfers between devices  2.95 us (7%)
  other arithmetic  0.62 us (2%)
    ppermute x10, starting transfers between devices, exchange(): return lax.ppermute(x, 'subj', [(i, i ^ mask) for i in range(n_subj)])  13.3 us
    all_to_all x1, blocking collectives, per_device(): sums = lax.all_to_all(sums, ('perm', 'subj'), 0, 0, tiled=True)  11.1 us
    pallas_call x5, Pallas kernels, call(): pl.pallas_call(body, out_shape=[space(shape, dtype) for space, (shape, dt...  9.46 us
    all_to_all x1, starting transfers between devices, per_device(): shuffles = lax.all_to_all(everyone, ('perm', 'subj'), 0, 0, tiled=True)  3.49 us
    ppermute x10, waiting for transfers between devices, exchange(): return lax.ppermute(x, 'subj', [(i, i ^ mask) for i in range(n_subj)])  1.85 us
    all_to_all x1, waiting for transfers between devices, per_device(): shuffles = lax.all_to_all(everyone, ('perm', 'subj'), 0, 0, tiled=True)  1.1 us
  transfers between devices with their start and end apart: 11, of which 2 were waited for; matrix products, arithmetic and copies ran while one was open for 0% of the time, Pallas kernels for 14%

profile of v4, /device:TPU:0, one launch (start us, length us, event | category | flops | bytes accessed | tf_op | source)
XLA Modules:
  0.0 41.0 jit_solution(14586377233301731760)
XLA Ops:
  0.0 1.3 %shard_map.37 = (s32[16,8,128]{2,1,0:T(8,128)}, bf16[256,256]{1,0:T(8,128)(2,1)S(1)}, bf16[256,256]{1,0:T(8,128)(2,1)S(1)}) custom-call(bf16[256,1024]{1,0:T(8,128)(2,1)} %phen_ref.1, s32[1,256]{1,0:T(1,128)} %bitcast.8), custom_call_target="tpu_custom_call" | custom-call | bytes 525312 | tf_op jit(solution)/shard_map/pallas_call | solution.py:23
  1.4 0.5 %collective-permute-start = (bf16[256,256]{1,0:T(8,128)(2,1)S(1)}, bf16[256,256]{1,0:T(8,128)(2,1)S(1)}, u32[]{:S(2)}, u32[]{:S(2)}) collective-permute-start(bf16[256,256]{1,0:T(8,128)(2,1)S(1)} %get-tuple-element.20), channel_id=1, source_target_pairs={{0,2},{2,0},{4,6},{6,4},{8,10},{10,8},{12,14},{14,12},{1,3},{3,1},... | collective-permute-start | bytes 393224 | tf_op jit(solution)/shard_map/ppermute | solution.py:183
  1.9 3.7 %collective-permute-start.3 = (bf16[256,256]{1,0:T(8,128)(2,1)S(1)}, bf16[256,256]{1,0:T(8,128)(2,1)S(1)}, u32[]{:S(2)}, u32[]{:S(2)}) collective-permute-start(bf16[256,256]{1,0:T(8,128)(2,1)S(1)} %get-tuple-element.21.refs_0_), channel_id=1, source_target_pairs={{0,8},{2,10},{4,12},{6,14},{8,0},{10,2},{12,4},{14,6},{1,9},{3,11}... | collective-permute-start | bytes 393224 | tf_op jit(solution)/shard_map/ppermute | solution.py:183
  5.5 1.6 %collective-permute-start.5 = (bf16[256,256]{1,0:T(8,128)(2,1)S(1)}, bf16[256,256]{1,0:T(8,128)(2,1)S(1)}, u32[]{:S(2)}, u32[]{:S(2)}) collective-permute-start(bf16[256,256]{1,0:T(8,128)(2,1)S(1)} %get-tuple-element.21.refs_0_), channel_id=1, source_target_pairs={{0,4},{2,6},{4,0},{6,2},{8,12},{10,14},{12,8},{14,10},{1,5},{3,7},... | collective-permute-start | bytes 393224 | tf_op jit(solution)/shard_map/ppermute | solution.py:183
  7.1 3.5 %all-to-all-start = ((s32[16,8,128]{2,1,0:T(8,128)}), s32[16,8,128]{2,1,0:T(8,128)S(1)}, u32[]{:S(2)}, u32[]{:S(2)}) async-start(s32[16,8,128]{2,1,0:T(8,128)} %get-tuple-element.19), calls=%async_computation | async-start | bytes 131072 | tf_op jit(solution)/shard_map/all_to_all | solution.py:217
  10.6 0.0 collective-permute-done.refs_1_
  10.6 1.9 %collective-permute-start.2 = (bf16[256,256]{1,0:T(8,128)(2,1)S(1)}, bf16[256,256]{1,0:T(8,128)(2,1)S(1)}, u32[]{:S(2)}, u32[]{:S(2)}) collective-permute-start(bf16[256,256]{1,0:T(8,128)(2,1)S(1)} %collective-permute-done.refs_1_), channel_id=1, source_target_pairs={{0,4},{2,6},{4,0},{6,2},{8,12},{10,14},{12,8},{14,10},{1,5},{3,7},... | collective-permute-start | bytes 393224 | tf_op jit(solution)/shard_map/ppermute | solution.py:183
  12.5 2.4 %collective-permute-start.1 = (bf16[256,256]{1,0:T(8,128)(2,1)S(1)}, bf16[256,256]{1,0:T(8,128)(2,1)S(1)}, u32[]{:S(2)}, u32[]{:S(2)}) collective-permute-start(bf16[256,256]{1,0:T(8,128)(2,1)S(1)} %collective-permute-done.refs_1_), channel_id=1, source_target_pairs={{0,8},{2,10},{4,12},{6,14},{8,0},{10,2},{12,4},{14,6},{1,9},{3,11}... | collective-permute-start | bytes 393224 | tf_op jit(solution)/shard_map/ppermute | solution.py:183
  14.9 0.0 collective-permute-done.3.refs_2_
  14.9 0.6 %collective-permute-start.4 = (bf16[256,256]{1,0:T(8,128)(2,1)S(1)}, bf16[256,256]{1,0:T(8,128)(2,1)S(1)}, u32[]{:S(2)}, u32[]{:S(2)}) collective-permute-start(bf16[256,256]{1,0:T(8,128)(2,1)S(1)} %collective-permute-done.3.refs_2_), channel_id=1, source_target_pairs={{0,4},{2,6},{4,0},{6,2},{8,12},{10,14},{12,8},{14,10},{1,5},{3,7},... | collective-permute-start | bytes 393224 | tf_op jit(solution)/shard_map/ppermute | solution.py:183
  15.4 1.4 %shard_map.40 = (bf16[256,2048]{1,0:T(8,128)(2,1)S(1)}, bf16[256,768]{1,0:T(8,128)(2,1)S(1)}, bf16[256,768]{1,0:T(8,128)(2,1)S(1)}, bf16[256,512]{1,0:T(8,128)(2,1)S(1)}) custom-call(bf16[256,2048]{1,0:T(8,128)(2,1)} %kin_ref.1), custom_call_target="tpu_custom_call" | custom-call | bytes 1048576 | tf_op jit(solution)/shard_map/pallas_call | solution.py:23
  16.8 1.1 %all-to-all-done.shuffle_ref = s32[16,8,128]{2,1,0:T(8,128)S(1)} async-done(((s32[16,8,128]{2,1,0:T(8,128)}), s32[16,8,128]{2,1,0:T(8,128)S(1)}, u32[]{:S(2)}, u32[]{:S(2)}) %all-to-all-start) | async-done | bytes 65568 | tf_op jit(solution)/shard_map/all_to_all | solution.py:217
  17.9 0.0 collective-permute-start.8
  17.9 0.0 collective-permute-done.5.refs_3_
  18.0 0.5 %collective-permute-start.7 = (bf16[256,768]{1,0:T(8,128)(2,1)S(1)}, bf16[256,768]{1,0:T(8,128)(2,1)S(1)}, u32[]{:S(2)}, u32[]{:S(2)}) collective-permute-start(bf16[256,768]{1,0:T(8,128)(2,1)S(1)} %get-tuple-element.28), channel_id=1, source_target_pairs={{0,2},{2,0},{4,6},{6,4},{8,10},{10,8},{12,14},{14,12},{1,3},{3,1},... | collective-permute-start | bytes 1179656 | tf_op jit(solution)/shard_map/ppermute | solution.py:183
  18.5 2.4 %shard_map.38 = (bf16[4096,256]{1,0:T(8,128)(2,1)S(1)}, f32[1,256]{1,0:T(1,128)S(1)}) custom-call(s32[16,8,128]{2,1,0:T(8,128)S(1)} %all-to-all-done.shuffle_ref, bf16[256,256]{1,0:T(8,128)(2,1)S(1)} %get-tuple-element.21.refs_0_, bf16[256,256]{1,0:T(8,128)(2,1)S(1)} %collective-permute-done.refs_1_, bf16[256,256]{1,0:T(8,128)(2,1)S(1)} %collective-permute-done.3.refs_2_, ...), custom_call_target="tpu_custom_call" | custom-call | tf_op jit(solution)/shard_map/pallas_call | solution.py:23
  20.9 0.0 collective-permute-done.2.refs_1_
  20.9 0.1 collective-permute-start.9
  21.0 0.0 collective-permute-done.1.refs_0_
  21.0 2.2 %collective-permute-start.6 = (bf16[256,256]{1,0:T(8,128)(2,1)S(1)}, bf16[256,256]{1,0:T(8,128)(2,1)S(1)}, u32[]{:S(2)}, u32[]{:S(2)}) collective-permute-start(bf16[256,256]{1,0:T(8,128)(2,1)S(1)} %collective-permute-done.1.refs_0_), channel_id=1, source_target_pairs={{0,4},{2,6},{4,0},{6,2},{8,12},{10,14},{12,8},{14,10},{1,5},{3,7},... | collective-permute-start | bytes 393224 | tf_op jit(solution)/shard_map/ppermute | solution.py:183
  23.2 0.0 collective-permute-done.4.refs_2_
  23.2 1.9 %shard_map.39 = (bf16[4096,256]{1,0:T(8,128)(2,1)S(1)}, f32[1,256]{1,0:T(1,128)S(1)}) custom-call(s32[16,8,128]{2,1,0:T(8,128)S(1)} %all-to-all-done.shuffle_ref, bf16[256,256]{1,0:T(8,128)(2,1)S(1)} %collective-permute-done.1.refs_0_, bf16[256,256]{1,0:T(8,128)(2,1)S(1)} %collective-permute-done.2.refs_1_, ...), custom_call_target="tpu_custom_call" | custom-call | flops 3758096384 | bytes 2556928 | tf_op jit(solution)/shard_map/pallas_call | solution.py:23
  25.1 0.0 collective-permute-done.9.refs_2_
  25.1 1.8 %collective-permute-done.6.last_ref = bf16[256,256]{1,0:T(8,128)(2,1)S(1)} collective-permute-done((bf16[256,256]{1,0:T(8,128)(2,1)S(1)}, bf16[256,256]{1,0:T(8,128)(2,1)S(1)}, u32[]{:S(2)}, u32[]{:S(2)}) %collective-permute-start.6) | collective-permute-done | bytes 131104 | tf_op jit(solution)/shard_map/ppermute | solution.py:183
  26.9 0.0 collective-permute-done.8.refs_1_
  26.9 0.0 collective-permute-done.7.refs_0_
  26.9 2.4 %shard_map.41 = f32[16,8,128]{2,1,0:T(8,128)S(1)} custom-call(s32[16,8,128]{2,1,0:T(8,128)S(1)} %all-to-all-done.shuffle_ref, bf16[4096,256]{1,0:T(8,128)(2,1)S(1)} %get-tuple-element.24.moved_ref, f32[1,256]{1,0:T(1,128)S(1)} %get-tuple-element.25.squares_ref, bf16[256,2048]{1,0:T(8,128)(2,1)S(1)} %get-tuple-element.26.own_ref, ...), custom_call_target="tpu_custom_call" | custom-call | flops 1610612736 | bytes 4391936 | tf_op jit(solution)/shard_map/pallas_call | solution.py:23
  29.3 11.1 %all_to_all.10 = f32[16,8,128]{2,1,0:T(8,128)S(1)} all-to-all(f32[16,8,128]{2,1,0:T(8,128)S(1)} %shard_map.41), channel_id=1, replica_groups=mesh['perm'=2,'subj'=8,'vert'=2] {'perm','subj'}, dimensions={0} | all-to-all | bytes 131072 | tf_op jit(solution)/shard_map/all_to_all | solution.py:261
  40.4 0.6 %div.12 = f32[1024]{0:T(1024)} divide(f32[1024]{0:T(1024)S(1)} %bitcast.6, f32[1024]{0:T(1024)S(1)} %bitcast.7) | non-fusion elementwise | flops 1024 | bytes 12288 | tf_op jit(solution)/shard_map/div | solution.py:267
  (2 shorter events, 0.0 us)
Async XLA Ops:
  1.4 9.3 %collective-permute-start = (bf16[256,256]{1,0:T(8,128)(2,1)S(1)}, bf16[256,256]{1,0:T(8,128)(2,1)S(1)}, u32[]{:S(2)}, u32[]{:S(2)}) collective-permute-start(bf16[256,256]{1,0:T(8,128)(2,1)S(1)} %get-tuple-element.20), channel_id=1, source_target_pairs={{0,2},{2,0},{4,6},{6,4},{8,10},{10,8},{12,14},{14,12},{1,3},{3,1},... | collective-permute-start | bytes 393224 | tf_op jit(solution)/shard_map/ppermute | solution.py:183
  1.9 13.0 %collective-permute-start.3 = (bf16[256,256]{1,0:T(8,128)(2,1)S(1)}, bf16[256,256]{1,0:T(8,128)(2,1)S(1)}, u32[]{:S(2)}, u32[]{:S(2)}) collective-permute-start(bf16[256,256]{1,0:T(8,128)(2,1)S(1)} %get-tuple-element.21.refs_0_), channel_id=1, source_target_pairs={{0,8},{2,10},{4,12},{6,14},{8,0},{10,2},{12,4},{14,6},{1,9},{3,11}... | collective-permute-start | bytes 393224 | tf_op jit(solution)/shard_map/ppermute | solution.py:183
  5.5 12.4 %collective-permute-start.5 = (bf16[256,256]{1,0:T(8,128)(2,1)S(1)}, bf16[256,256]{1,0:T(8,128)(2,1)S(1)}, u32[]{:S(2)}, u32[]{:S(2)}) collective-permute-start(bf16[256,256]{1,0:T(8,128)(2,1)S(1)} %get-tuple-element.21.refs_0_), channel_id=1, source_target_pairs={{0,4},{2,6},{4,0},{6,2},{8,12},{10,14},{12,8},{14,10},{1,5},{3,7},... | collective-permute-start | bytes 393224 | tf_op jit(solution)/shard_map/ppermute | solution.py:183
  7.1 10.8 %all-to-all-start = ((s32[16,8,128]{2,1,0:T(8,128)}), s32[16,8,128]{2,1,0:T(8,128)S(1)}, u32[]{:S(2)}, u32[]{:S(2)}) async-start(s32[16,8,128]{2,1,0:T(8,128)} %get-tuple-element.19), calls=%async_computation | async-start | bytes 131072 | tf_op jit(solution)/shard_map/all_to_all | solution.py:217
  10.6 10.3 %collective-permute-start.2 = (bf16[256,256]{1,0:T(8,128)(2,1)S(1)}, bf16[256,256]{1,0:T(8,128)(2,1)S(1)}, u32[]{:S(2)}, u32[]{:S(2)}) collective-permute-start(bf16[256,256]{1,0:T(8,128)(2,1)S(1)} %collective-permute-done.refs_1_), channel_id=1, source_target_pairs={{0,4},{2,6},{4,0},{6,2},{8,12},{10,14},{12,8},{14,10},{1,5},{3,7},... | collective-permute-start | bytes 393224 | tf_op jit(solution)/shard_map/ppermute | solution.py:183
  12.5 8.5 %collective-permute-start.1 = (bf16[256,256]{1,0:T(8,128)(2,1)S(1)}, bf16[256,256]{1,0:T(8,128)(2,1)S(1)}, u32[]{:S(2)}, u32[]{:S(2)}) collective-permute-start(bf16[256,256]{1,0:T(8,128)(2,1)S(1)} %collective-permute-done.refs_1_), channel_id=1, source_target_pairs={{0,8},{2,10},{4,12},{6,14},{8,0},{10,2},{12,4},{14,6},{1,9},{3,11}... | collective-permute-start | bytes 393224 | tf_op jit(solution)/shard_map/ppermute | solution.py:183
  14.9 8.3 %collective-permute-start.4 = (bf16[256,256]{1,0:T(8,128)(2,1)S(1)}, bf16[256,256]{1,0:T(8,128)(2,1)S(1)}, u32[]{:S(2)}, u32[]{:S(2)}) collective-permute-start(bf16[256,256]{1,0:T(8,128)(2,1)S(1)} %collective-permute-done.3.refs_2_), channel_id=1, source_target_pairs={{0,4},{2,6},{4,0},{6,2},{8,12},{10,14},{12,8},{14,10},{1,5},{3,7},... | collective-permute-start | bytes 393224 | tf_op jit(solution)/shard_map/ppermute | solution.py:183
  17.9 9.0 %collective-permute-start.8 = (bf16[256,768]{1,0:T(8,128)(2,1)S(1)}, bf16[256,768]{1,0:T(8,128)(2,1)S(1)}, u32[]{:S(2)}, u32[]{:S(2)}) collective-permute-start(bf16[256,768]{1,0:T(8,128)(2,1)S(1)} %get-tuple-element.30), channel_id=1, source_target_pairs={{0,2},{2,0},{4,6},{6,4},{8,10},{10,8},{12,14},{14,12},{1,3},{3,1},... | collective-permute-start | bytes 1179656 | tf_op jit(solution)/shard_map/ppermute | solution.py:183
  18.0 9.0 %collective-permute-start.7 = (bf16[256,768]{1,0:T(8,128)(2,1)S(1)}, bf16[256,768]{1,0:T(8,128)(2,1)S(1)}, u32[]{:S(2)}, u32[]{:S(2)}) collective-permute-start(bf16[256,768]{1,0:T(8,128)(2,1)S(1)} %get-tuple-element.28), channel_id=1, source_target_pairs={{0,2},{2,0},{4,6},{6,4},{8,10},{10,8},{12,14},{14,12},{1,3},{3,1},... | collective-permute-start | bytes 1179656 | tf_op jit(solution)/shard_map/ppermute | solution.py:183
  20.9 4.2 %collective-permute-start.9 = (bf16[256,512]{1,0:T(8,128)(2,1)S(1)}, bf16[256,512]{1,0:T(8,128)(2,1)S(1)}, u32[]{:S(2)}, u32[]{:S(2)}) collective-permute-start(bf16[256,512]{1,0:T(8,128)(2,1)S(1)} %get-tuple-element.32), channel_id=1, source_target_pairs={{0,2},{2,0},{4,6},{6,4},{8,10},{10,8},{12,14},{14,12},{1,3},{3,1},... | collective-permute-start | bytes 786440 | tf_op jit(solution)/shard_map/ppermute | solution.py:183
  21.0 5.9 %collective-permute-start.6 = (bf16[256,256]{1,0:T(8,128)(2,1)S(1)}, bf16[256,256]{1,0:T(8,128)(2,1)S(1)}, u32[]{:S(2)}, u32[]{:S(2)}) collective-permute-start(bf16[256,256]{1,0:T(8,128)(2,1)S(1)} %collective-permute-done.1.refs_0_), channel_id=1, source_target_pairs={{0,4},{2,6},{4,0},{6,2},{8,12},{10,14},{12,8},{14,10},{1,5},{3,7},... | collective-permute-start | bytes 393224 | tf_op jit(solution)/shard_map/ppermute | solution.py:183

commit v5 on v4

--- a/solution.py
+++ b/solution.py
@@ -151,7 +151,28 @@
     squares_ref[...] = before[1][...] + squares if before else squares
 
 
-def finish(order, perms, shuffle_ref, moved_ref, squares_ref, own_ref, last_ref, *refs):
+def weigh(order, perms, shuffle_ref, own_ref, weights_ref):
+    rows, me = own_ref.shape[0], lax.axis_index("subj")
+    for p in range(perms):
+        picks = []
+        for source in order:
+            digits = columns_of(shuffle_ref, p, me ^ source, perms, rows)
+            picks.append(picker(digits, me ^ order[-1], rows))
+        picks = jnp.concatenate(picks, axis=0)
+        weights_ref[tile(p, rows), :] = dot(own_ref[...], picks).astype(BF16)
+
+
+def multiply(perms, moved_ref, own_ref, product_ref):
+    rows = own_ref.shape[0]
+    subjects = moved_ref.shape[0] // perms
+    for p in range(perms):
+        x = moved_ref[tile(p, subjects), :]
+        product_ref[tile(p, rows), :] = dot(own_ref[...], x)
+
+
+def finish(
+    order, perms, shuffle_ref, moved_ref, squares_ref, weights_ref, product_ref, last_ref, *refs
+):
     sib_refs, (out_ref, full_ref) = refs[:-2], refs[-2:]
     rows, me = last_ref.shape[0], lax.axis_index("subj")
     n = len(order)
@@ -163,8 +184,10 @@
             digits = columns_of(shuffle_ref, p, me ^ order[i], perms, rows)
             found = find(order[-1:], [last_ref], digits, rows)
             full_ref[tile(i, rows), :] = moved_ref[tile(p * n + i, rows), :] + found
+        more = dot(weights_ref[tile(p, rows), :], last_ref[...])
+        products = [product_ref[tile(p, rows), :] + more, times(sib_refs, full_ref)]
         cross = jnp.zeros_like(squares)
-        for g, product in enumerate([dot(own_ref[...], full_ref[...]), times(sib_refs, full_ref)]):
+        for g, product in enumerate(products):
             mine = full_ref[tile(g, rows), :].astype(F32)
             cross += jnp.sum(mine * product, axis=0, keepdims=True)
         lines = [cross[:, h * LANES : (h + 1) * LANES] for h in range(halves)]
@@ -246,13 +269,28 @@
         squares,
         flops=unit * tiles * (n_subj - 1),
     )
+    weights = call(
+        functools.partial(weigh, order, n_perm),
+        [((n_perm * rows, rows), BF16)],
+        shuffles,
+        own_kin,
+        size=0,
+    )[0]
+    product = call(
+        functools.partial(multiply, n_perm),
+        [((n_perm * rows, width), F32)],
+        moved,
+        own_kin,
+        size=0,
+    )[0]
     sums = call(
         functools.partial(finish, order, n_perm),
         [((tiles, 8, LANES), F32)],
         shuffles,
         moved,
         squares,
-        own_kin,
+        weights,
+        product,
         chunks[-1],
         *sib_kin,
         flops=unit * tiles * 3,

time: 41.3 us -> 40.8 us (0.988)
  Pallas kernels: 9.46 us -> 10.9 us
  starting transfers between devices: 16.8 us -> 15.5 us
  blocking collectives: 11.1 us -> 9.8 us
  waiting for transfers between devices: 2.95 us -> 3.49 us
    pallas_call x5 -> x7, Pallas kernels: 9.46 us -> 10.9 us  [call(): pl.pallas_call(body, out_shape=[space(shape, dtype) for space, (shape, dt...]
    all_to_all x1, blocking collectives: 11.1 us -> 9.8 us  [per_device(): sums = lax.all_to_all(sums, ('perm', 'subj'), 0, 0, tiled=True)]
    ppermute x10, starting transfers between devices: 13.3 us -> 12.1 us  [exchange(): return lax.ppermute(x, 'subj', [(i, i ^ mask) for i in range(n_subj)])]
    ppermute x10, waiting for transfers between devices: 1.85 us -> 2.4 us  [exchange(): return lax.ppermute(x, 'subj', [(i, i ^ mask) for i in range(n_subj)])]
  transfers between devices with their start and end apart: 11 -> 11, of which waited for: 2 -> 2; matrix products, arithmetic and copies ran while one was open for 0% -> 0% of each run, Pallas kernels for 14% -> 19%
where the time goes in v5:
time: 40.8 us; the launch traced here: 40.5 us
  starting transfers between devices  15.5 us (38%)
  Pallas kernels  10.9 us (27%)
  blocking collectives  9.8 us (24%)
  waiting for transfers between devices  3.49 us (9%)
  other arithmetic  0.62 us (2%)
    ppermute x10, starting transfers between devices, exchange(): return lax.ppermute(x, 'subj', [(i, i ^ mask) for i in range(n_subj)])  12.1 us
    pallas_call x7, Pallas kernels, call(): pl.pallas_call(body, out_shape=[space(shape, dtype) for space, (shape, dt...  10.9 us
    all_to_all x1, blocking collectives, per_device(): sums = lax.all_to_all(sums, ('perm', 'subj'), 0, 0, tiled=True)  9.8 us
    all_to_all x1, starting transfers between devices, per_device(): shuffles = lax.all_to_all(everyone, ('perm', 'subj'), 0, 0, tiled=True)  3.49 us
    ppermute x10, waiting for transfers between devices, exchange(): return lax.ppermute(x, 'subj', [(i, i ^ mask) for i in range(n_subj)])  2.4 us
    all_to_all x1, waiting for transfers between devices, per_device(): shuffles = lax.all_to_all(everyone, ('perm', 'subj'), 0, 0, tiled=True)  1.1 us
  transfers between devices with their start and end apart: 11, of which 2 were waited for; matrix products, arithmetic and copies ran while one was open for 0% of the time, Pallas kernels for 19%

profile of v5, /device:TPU:0, one launch (start us, length us, event | category | flops | bytes accessed | tf_op | source)
XLA Modules:
  0.0 40.5 jit_solution(12210824194580861704)
XLA Ops:
  0.0 1.3 %shard_map.37 = (s32[16,8,128]{2,1,0:T(8,128)}, bf16[256,256]{1,0:T(8,128)(2,1)S(1)}, bf16[256,256]{1,0:T(8,128)(2,1)S(1)}) custom-call(bf16[256,1024]{1,0:T(8,128)(2,1)} %phen_ref.1, s32[1,256]{1,0:T(1,128)} %bitcast.8), custom_call_target="tpu_custom_call" | custom-call | bytes 525312 | tf_op jit(solution)/shard_map/pallas_call | solution.py:23
  1.4 0.5 %collective-permute-start = (bf16[256,256]{1,0:T(8,128)(2,1)S(1)}, bf16[256,256]{1,0:T(8,128)(2,1)S(1)}, u32[]{:S(2)}, u32[]{:S(2)}) collective-permute-start(bf16[256,256]{1,0:T(8,128)(2,1)S(1)} %get-tuple-element.20), channel_id=1, source_target_pairs={{0,2},{2,0},{4,6},{6,4},{8,10},{10,8},{12,14},{14,12},{1,3},{3,1},... | collective-permute-start | bytes 393224 | tf_op jit(solution)/shard_map/ppermute | solution.py:206
  1.9 3.7 %collective-permute-start.3 = (bf16[256,256]{1,0:T(8,128)(2,1)S(1)}, bf16[256,256]{1,0:T(8,128)(2,1)S(1)}, u32[]{:S(2)}, u32[]{:S(2)}) collective-permute-start(bf16[256,256]{1,0:T(8,128)(2,1)S(1)} %get-tuple-element.21.refs_0_), channel_id=1, source_target_pairs={{0,8},{2,10},{4,12},{6,14},{8,0},{10,2},{12,4},{14,6},{1,9},{3,11}... | collective-permute-start | bytes 393224 | tf_op jit(solution)/shard_map/ppermute | solution.py:206
  5.5 1.6 %collective-permute-start.5 = (bf16[256,256]{1,0:T(8,128)(2,1)S(1)}, bf16[256,256]{1,0:T(8,128)(2,1)S(1)}, u32[]{:S(2)}, u32[]{:S(2)}) collective-permute-start(bf16[256,256]{1,0:T(8,128)(2,1)S(1)} %get-tuple-element.21.refs_0_), channel_id=1, source_target_pairs={{0,4},{2,6},{4,0},{6,2},{8,12},{10,14},{12,8},{14,10},{1,5},{3,7},... | collective-permute-start | bytes 393224 | tf_op jit(solution)/shard_map/ppermute | solution.py:206
  7.1 3.5 %all-to-all-start = ((s32[16,8,128]{2,1,0:T(8,128)}), s32[16,8,128]{2,1,0:T(8,128)S(1)}, u32[]{:S(2)}, u32[]{:S(2)}) async-start(s32[16,8,128]{2,1,0:T(8,128)} %get-tuple-element.19), calls=%async_computation | async-start | bytes 131072 | tf_op jit(solution)/shard_map/all_to_all | solution.py:240
  10.6 0.0 collective-permute-done.refs_1_
  10.6 1.9 %collective-permute-start.2 = (bf16[256,256]{1,0:T(8,128)(2,1)S(1)}, bf16[256,256]{1,0:T(8,128)(2,1)S(1)}, u32[]{:S(2)}, u32[]{:S(2)}) collective-permute-start(bf16[256,256]{1,0:T(8,128)(2,1)S(1)} %collective-permute-done.refs_1_), channel_id=1, source_target_pairs={{0,4},{2,6},{4,0},{6,2},{8,12},{10,14},{12,8},{14,10},{1,5},{3,7},... | collective-permute-start | bytes 393224 | tf_op jit(solution)/shard_map/ppermute | solution.py:206
  12.5 2.4 %collective-permute-start.1 = (bf16[256,256]{1,0:T(8,128)(2,1)S(1)}, bf16[256,256]{1,0:T(8,128)(2,1)S(1)}, u32[]{:S(2)}, u32[]{:S(2)}) collective-permute-start(bf16[256,256]{1,0:T(8,128)(2,1)S(1)} %collective-permute-done.refs_1_), channel_id=1, source_target_pairs={{0,8},{2,10},{4,12},{6,14},{8,0},{10,2},{12,4},{14,6},{1,9},{3,11}... | collective-permute-start | bytes 393224 | tf_op jit(solution)/shard_map/ppermute | solution.py:206
  14.9 0.0 collective-permute-done.3.refs_2_
  14.9 0.6 %collective-permute-start.4 = (bf16[256,256]{1,0:T(8,128)(2,1)S(1)}, bf16[256,256]{1,0:T(8,128)(2,1)S(1)}, u32[]{:S(2)}, u32[]{:S(2)}) collective-permute-start(bf16[256,256]{1,0:T(8,128)(2,1)S(1)} %collective-permute-done.3.refs_2_), channel_id=1, source_target_pairs={{0,4},{2,6},{4,0},{6,2},{8,12},{10,14},{12,8},{14,10},{1,5},{3,7},... | collective-permute-start | bytes 393224 | tf_op jit(solution)/shard_map/ppermute | solution.py:206
  15.4 1.4 %shard_map.40 = (bf16[256,2048]{1,0:T(8,128)(2,1)S(1)}, bf16[256,768]{1,0:T(8,128)(2,1)S(1)}, bf16[256,768]{1,0:T(8,128)(2,1)S(1)}, bf16[256,512]{1,0:T(8,128)(2,1)S(1)}) custom-call(bf16[256,2048]{1,0:T(8,128)(2,1)} %kin_ref.1), custom_call_target="tpu_custom_call" | custom-call | bytes 1048576 | tf_op jit(solution)/shard_map/pallas_call | solution.py:23
  16.8 1.1 %all-to-all-done.shuffle_ref = s32[16,8,128]{2,1,0:T(8,128)S(1)} async-done(((s32[16,8,128]{2,1,0:T(8,128)}), s32[16,8,128]{2,1,0:T(8,128)S(1)}, u32[]{:S(2)}, u32[]{:S(2)}) %all-to-all-start) | async-done | bytes 65568 | tf_op jit(solution)/shard_map/all_to_all | solution.py:240
  17.9 0.0 collective-permute-start.8
  17.9 0.0 collective-permute-done.5.refs_3_
  18.0 0.5 %collective-permute-start.7 = (bf16[256,768]{1,0:T(8,128)(2,1)S(1)}, bf16[256,768]{1,0:T(8,128)(2,1)S(1)}, u32[]{:S(2)}, u32[]{:S(2)}) collective-permute-start(bf16[256,768]{1,0:T(8,128)(2,1)S(1)} %get-tuple-element.28), channel_id=1, source_target_pairs={{0,2},{2,0},{4,6},{6,4},{8,10},{10,8},{12,14},{14,12},{1,3},{3,1},... | collective-permute-start | bytes 1179656 | tf_op jit(solution)/shard_map/ppermute | solution.py:206
  18.5 1.2 %shard_map.41.weights_ref = bf16[512,256]{1,0:T(8,128)(2,1)S(1)} custom-call(s32[16,8,128]{2,1,0:T(8,128)S(1)} %all-to-all-done.shuffle_ref, bf16[256,2048]{1,0:T(8,128)(2,1)S(1)} %get-tuple-element.26.own_ref), custom_call_target="tpu_custom_call" | custom-call | tf_op jit(solution)/shard_map/pallas_call | solution.py:23
  19.7 2.4 %shard_map.38 = (bf16[4096,256]{1,0:T(8,128)(2,1)S(1)}, f32[1,256]{1,0:T(1,128)S(1)}) custom-call(s32[16,8,128]{2,1,0:T(8,128)S(1)} %all-to-all-done.shuffle_ref, bf16[256,256]{1,0:T(8,128)(2,1)S(1)} %get-tuple-element.21.refs_0_, bf16[256,256]{1,0:T(8,128)(2,1)S(1)} %collective-permute-done.refs_1_, bf16[256,256]{1,0:T(8,128)(2,1)S(1)} %collective-permute-done.3.refs_2_, ...), custom_call_target="tpu_custom_call" | custom-call | tf_op jit(solution)/shard_map/pallas_call | solution.py:23
  22.2 0.0 collective-permute-done.2.refs_1_
  22.2 0.1 collective-permute-start.9
  22.2 0.0 collective-permute-done.1.refs_0_
  22.3 0.9 %collective-permute-start.6 = (bf16[256,256]{1,0:T(8,128)(2,1)S(1)}, bf16[256,256]{1,0:T(8,128)(2,1)S(1)}, u32[]{:S(2)}, u32[]{:S(2)}) collective-permute-start(bf16[256,256]{1,0:T(8,128)(2,1)S(1)} %collective-permute-done.1.refs_0_), channel_id=1, source_target_pairs={{0,4},{2,6},{4,0},{6,2},{8,12},{10,14},{12,8},{14,10},{1,5},{3,7},... | collective-permute-start | bytes 393224 | tf_op jit(solution)/shard_map/ppermute | solution.py:206
  23.2 0.0 collective-permute-done.4.refs_2_
  23.2 1.9 %shard_map.39 = (bf16[4096,256]{1,0:T(8,128)(2,1)S(1)}, f32[1,256]{1,0:T(1,128)S(1)}) custom-call(s32[16,8,128]{2,1,0:T(8,128)S(1)} %all-to-all-done.shuffle_ref, bf16[256,256]{1,0:T(8,128)(2,1)S(1)} %collective-permute-done.1.refs_0_, bf16[256,256]{1,0:T(8,128)(2,1)S(1)} %collective-permute-done.2.refs_1_, ...), custom_call_target="tpu_custom_call" | custom-call | flops 3758096384 | bytes 2556928 | tf_op jit(solution)/shard_map/pallas_call | solution.py:23
  25.1 0.7 %shard_map.42.product_ref = f32[512,256]{1,0:T(8,128)S(1)} custom-call(bf16[4096,256]{1,0:T(8,128)(2,1)S(1)} %get-tuple-element.24.moved_ref, bf16[256,2048]{1,0:T(8,128)(2,1)S(1)} %get-tuple-element.26.own_ref), custom_call_target="tpu_custom_call" | custom-call | tf_op jit(solution)/shard_map/pallas_call | solution.py:23
  25.8 0.0 collective-permute-done.9.refs_2_
  25.8 2.4 %collective-permute-done.6.last_ref = bf16[256,256]{1,0:T(8,128)(2,1)S(1)} collective-permute-done((bf16[256,256]{1,0:T(8,128)(2,1)S(1)}, bf16[256,256]{1,0:T(8,128)(2,1)S(1)}, u32[]{:S(2)}, u32[]{:S(2)}) %collective-permute-start.6) | collective-permute-done | bytes 131104 | tf_op jit(solution)/shard_map/ppermute | solution.py:206
  28.2 0.0 collective-permute-done.8.refs_1_
  28.2 0.0 collective-permute-done.7.refs_0_
  28.2 1.9 %shard_map.43 = f32[16,8,128]{2,1,0:T(8,128)S(1)} custom-call(s32[16,8,128]{2,1,0:T(8,128)S(1)} %all-to-all-done.shuffle_ref, bf16[4096,256]{1,0:T(8,128)(2,1)S(1)} %get-tuple-element.24.moved_ref, f32[1,256]{1,0:T(1,128)S(1)} %get-tuple-element.25.squares_ref, bf16[512,256]{1,0:T(8,128)(2,1)S(1)} %shard_map.41.weights_ref, ...), custom_call_target="tpu_custom_call" | custom-call | flops 1610612736 | bytes 4129792 | tf_op jit(solution)/shard_map/pallas_call | solution.py:23
  30.1 9.8 %all_to_all.10 = f32[16,8,128]{2,1,0:T(8,128)S(1)} all-to-all(f32[16,8,128]{2,1,0:T(8,128)S(1)} %shard_map.43), channel_id=1, replica_groups=mesh['perm'=2,'subj'=8,'vert'=2] {'perm','subj'}, dimensions={0} | all-to-all | bytes 131072 | tf_op jit(solution)/shard_map/all_to_all | solution.py:299
  39.9 0.6 %div.12 = f32[1024]{0:T(1024)} divide(f32[1024]{0:T(1024)S(1)} %bitcast.6, f32[1024]{0:T(1024)S(1)} %bitcast.7) | non-fusion elementwise | flops 1024 | bytes 12288 | tf_op jit(solution)/shard_map/div | solution.py:305
  (2 shorter events, 0.0 us)
Async XLA Ops:
  1.4 9.3 %collective-permute-start = (bf16[256,256]{1,0:T(8,128)(2,1)S(1)}, bf16[256,256]{1,0:T(8,128)(2,1)S(1)}, u32[]{:S(2)}, u32[]{:S(2)}) collective-permute-start(bf16[256,256]{1,0:T(8,128)(2,1)S(1)} %get-tuple-element.20), channel_id=1, source_target_pairs={{0,2},{2,0},{4,6},{6,4},{8,10},{10,8},{12,14},{14,12},{1,3},{3,1},... | collective-permute-start | bytes 393224 | tf_op jit(solution)/shard_map/ppermute | solution.py:206
  1.9 13.0 %collective-permute-start.3 = (bf16[256,256]{1,0:T(8,128)(2,1)S(1)}, bf16[256,256]{1,0:T(8,128)(2,1)S(1)}, u32[]{:S(2)}, u32[]{:S(2)}) collective-permute-start(bf16[256,256]{1,0:T(8,128)(2,1)S(1)} %get-tuple-element.21.refs_0_), channel_id=1, source_target_pairs={{0,8},{2,10},{4,12},{6,14},{8,0},{10,2},{12,4},{14,6},{1,9},{3,11}... | collective-permute-start | bytes 393224 | tf_op jit(solution)/shard_map/ppermute | solution.py:206
  5.5 12.4 %collective-permute-start.5 = (bf16[256,256]{1,0:T(8,128)(2,1)S(1)}, bf16[256,256]{1,0:T(8,128)(2,1)S(1)}, u32[]{:S(2)}, u32[]{:S(2)}) collective-permute-start(bf16[256,256]{1,0:T(8,128)(2,1)S(1)} %get-tuple-element.21.refs_0_), channel_id=1, source_target_pairs={{0,4},{2,6},{4,0},{6,2},{8,12},{10,14},{12,8},{14,10},{1,5},{3,7},... | collective-permute-start | bytes 393224 | tf_op jit(solution)/shard_map/ppermute | solution.py:206
  7.1 10.8 %all-to-all-start = ((s32[16,8,128]{2,1,0:T(8,128)}), s32[16,8,128]{2,1,0:T(8,128)S(1)}, u32[]{:S(2)}, u32[]{:S(2)}) async-start(s32[16,8,128]{2,1,0:T(8,128)} %get-tuple-element.19), calls=%async_computation | async-start | bytes 131072 | tf_op jit(solution)/shard_map/all_to_all | solution.py:240
  10.6 11.5 %collective-permute-start.2 = (bf16[256,256]{1,0:T(8,128)(2,1)S(1)}, bf16[256,256]{1,0:T(8,128)(2,1)S(1)}, u32[]{:S(2)}, u32[]{:S(2)}) collective-permute-start(bf16[256,256]{1,0:T(8,128)(2,1)S(1)} %collective-permute-done.refs_1_), channel_id=1, source_target_pairs={{0,4},{2,6},{4,0},{6,2},{8,12},{10,14},{12,8},{14,10},{1,5},{3,7},... | collective-permute-start | bytes 393224 | tf_op jit(solution)/shard_map/ppermute | solution.py:206
  12.5 9.8 %collective-permute-start.1 = (bf16[256,256]{1,0:T(8,128)(2,1)S(1)}, bf16[256,256]{1,0:T(8,128)(2,1)S(1)}, u32[]{:S(2)}, u32[]{:S(2)}) collective-permute-start(bf16[256,256]{1,0:T(8,128)(2,1)S(1)} %collective-permute-done.refs_1_), channel_id=1, source_target_pairs={{0,8},{2,10},{4,12},{6,14},{8,0},{10,2},{12,4},{14,6},{1,9},{3,11}... | collective-permute-start | bytes 393224 | tf_op jit(solution)/shard_map/ppermute | solution.py:206
  14.9 8.3 %collective-permute-start.4 = (bf16[256,256]{1,0:T(8,128)(2,1)S(1)}, bf16[256,256]{1,0:T(8,128)(2,1)S(1)}, u32[]{:S(2)}, u32[]{:S(2)}) collective-permute-start(bf16[256,256]{1,0:T(8,128)(2,1)S(1)} %collective-permute-done.3.refs_2_), channel_id=1, source_target_pairs={{0,4},{2,6},{4,0},{6,2},{8,12},{10,14},{12,8},{14,10},{1,5},{3,7},... | collective-permute-start | bytes 393224 | tf_op jit(solution)/shard_map/ppermute | solution.py:206
  17.9 10.2 %collective-permute-start.8 = (bf16[256,768]{1,0:T(8,128)(2,1)S(1)}, bf16[256,768]{1,0:T(8,128)(2,1)S(1)}, u32[]{:S(2)}, u32[]{:S(2)}) collective-permute-start(bf16[256,768]{1,0:T(8,128)(2,1)S(1)} %get-tuple-element.30), channel_id=1, source_target_pairs={{0,2},{2,0},{4,6},{6,4},{8,10},{10,8},{12,14},{14,12},{1,3},{3,1},... | collective-permute-start | bytes 1179656 | tf_op jit(solution)/shard_map/ppermute | solution.py:206
  18.0 10.2 %collective-permute-start.7 = (bf16[256,768]{1,0:T(8,128)(2,1)S(1)}, bf16[256,768]{1,0:T(8,128)(2,1)S(1)}, u32[]{:S(2)}, u32[]{:S(2)}) collective-permute-start(bf16[256,768]{1,0:T(8,128)(2,1)S(1)} %get-tuple-element.28), channel_id=1, source_target_pairs={{0,2},{2,0},{4,6},{6,4},{8,10},{10,8},{12,14},{14,12},{1,3},{3,1},... | collective-permute-start | bytes 1179656 | tf_op jit(solution)/shard_map/ppermute | solution.py:206
  22.2 3.6 %collective-permute-start.9 = (bf16[256,512]{1,0:T(8,128)(2,1)S(1)}, bf16[256,512]{1,0:T(8,128)(2,1)S(1)}, u32[]{:S(2)}, u32[]{:S(2)}) collective-permute-start(bf16[256,512]{1,0:T(8,128)(2,1)S(1)} %get-tuple-element.32), channel_id=1, source_target_pairs={{0,2},{2,0},{4,6},{6,4},{8,10},{10,8},{12,14},{14,12},{1,3},{3,1},... | collective-permute-start | bytes 786440 | tf_op jit(solution)/shard_map/ppermute | solution.py:206
  22.3 5.9 %collective-permute-start.6 = (bf16[256,256]{1,0:T(8,128)(2,1)S(1)}, bf16[256,256]{1,0:T(8,128)(2,1)S(1)}, u32[]{:S(2)}, u32[]{:S(2)}) collective-permute-start(bf16[256,256]{1,0:T(8,128)(2,1)S(1)} %collective-permute-done.1.refs_0_), channel_id=1, source_target_pairs={{0,4},{2,6},{4,0},{6,2},{8,12},{10,14},{12,8},{14,10},{1,5},{3,7},... | collective-permute-start | bytes 393224 | tf_op jit(solution)/shard_map/ppermute | solution.py:206
